TPU v7x, 256 devices: a whole 4x4x8 slice. The times are simulated.
256 devices in a mesh: plane: 4 (over x_lo, core), col: 64 (over x_hi, y, z).
Axes of the slice: x: 4 (x_hi: 2, x_lo: 2; x = x_hi * 2 + x_lo), y: 4, z: 8, core: 2. Of those that a mesh axis runs over, the one named last changes fastest.
Arguments:
- exposures: float32 [8, 1024, 16384], P('plane', None, 'col'), may hold values from -6 to 6
Outputs:
- joined: float32 [1024, 16384], P('plane', 'col')
All inputs are finite; a program needn't handle non-finite values.
Results may differ from a plain program's by a relative error of at most 0.00002.
Values sent between devices are 32-bit elements; how exact they have to be, the bound alone decides.
A program may use at most 128 MiB of HBM per device.

v0:
```python
import jax
import jax.numpy as jnp
from jax import lax
from jax.sharding import PartitionSpec as P

P_SIZE = 8


FILTER_TAPS = (0.0625, 0.25, 0.375, 0.25, 0.0625)


def with_halo(block, sides, width):
    for axis, dim in sides:
        count = lax.axis_size(axis)
        forward = [(i, i + 1) for i in range(count - 1)]
        backward = [(target, source) for source, target in forward]
        low = lax.ppermute(
            lax.slice_in_dim(block, block.shape[dim] - width, None, axis=dim), axis, forward
        )
        high = lax.ppermute(lax.slice_in_dim(block, 0, width, axis=dim), axis, backward)
        block = jnp.concatenate([low, block, high], axis=dim)
    return block


def pad_axis(values, along, margin):
    widths = [(0, 0)] * values.ndim
    widths[along] = (margin, margin)
    return jnp.pad(values, widths)


def reduce_along(padded, along, amount):
    summed = FILTER_TAPS[0] * lax.slice_in_dim(padded, 0, 2 * amount - 1, 2, along)
    for offset in range(1, 5):
        summed = summed + FILTER_TAPS[offset] * lax.slice_in_dim(
            padded, offset, offset + 2 * amount - 1, 2, along
        )
    return summed


def expand_along(padded, along, amount):
    first = lax.slice_in_dim(padded, 0, amount, 1, along)
    second = lax.slice_in_dim(padded, 1, amount + 1, 1, along)
    third = lax.slice_in_dim(padded, 2, amount + 2, 1, along)
    even = (
        2.0 * FILTER_TAPS[0] * first + 2.0 * FILTER_TAPS[2] * second + 2.0 * FILTER_TAPS[4] * third
    )
    odd = 2.0 * FILTER_TAPS[1] * second + 2.0 * FILTER_TAPS[3] * third
    new_shape = list(even.shape)
    new_shape[along] = 2 * amount
    return jnp.stack([even, odd], axis=along + 1).reshape(new_shape)


def height_op(values, reducing):
    amount = values.shape[1]
    if reducing:
        return reduce_along(pad_axis(values, 1, 2), 1, amount // 2)
    return expand_along(pad_axis(values, 1, 1), 1, amount)


def energy_logit(detail):
    squared = detail * detail
    return 4.0 * squared / (1.0 + squared)


def width_op(values, reducing):
    strip = lax.all_to_all(values, "col", split_axis=1, concat_axis=2, tiled=True)
    length = strip.shape[2]
    if reducing:
        result = reduce_along(pad_axis(strip, 2, 2), 2, length // 2)
    else:
        result = expand_along(pad_axis(strip, 2, 1), 2, length)
    return lax.all_to_all(result, "col", split_axis=2, concat_axis=1, tiled=True)


def body(exposures):
    half_rows = height_op(exposures, True)
    coarse_one = width_op(half_rows, True)
    widened = width_op(coarse_one, False)
    detail_zero = exposures - height_op(widened, False)
    quarter_rows = height_op(coarse_one, True)
    coarse_two = width_op(quarter_rows, True)
    widened_two = width_op(coarse_two, False)
    base_two = height_op(widened_two, False)
    detail_one = coarse_one - base_two
    level_zero, level_one, level_base = (
        lax.all_to_all(detail_zero, "plane", split_axis=1, concat_axis=0, tiled=True),
        lax.all_to_all(detail_one, "plane", split_axis=1, concat_axis=0, tiled=True),
        lax.all_to_all(base_two, "plane", split_axis=1, concat_axis=0, tiled=True),
    )
    weight_zero = jnp.exp(energy_logit(level_zero))
    weight_one = jnp.exp(energy_logit(level_one))
    joined_zero = jnp.sum(weight_zero * level_zero, axis=0) / jnp.sum(weight_zero, axis=0)
    joined_detail = jnp.sum(weight_one * level_one, axis=0) / jnp.sum(weight_one, axis=0)
    base_sum = jnp.sum(level_base, axis=0)
    joined_one = joined_detail + base_sum / P_SIZE
    margin = with_halo(joined_one, (("plane", 0), ("col", 1)), 1)
    row_count = joined_one.shape[0]
    column_count = joined_one.shape[1]
    rows_up = expand_along(margin, 0, row_count)
    return joined_zero + expand_along(rows_up, 1, column_count)


def solution(mesh):
    in_specs = (P("plane", None, "col"),)
    out_specs = P("plane", "col")
    return jax.shard_map(body, mesh=mesh, in_specs=in_specs, out_specs=out_specs, check_vma=False)
```

profile of v0, /device:TPU:2, one launch (start us, length us, event | category | flops | bytes accessed | tf_op | source)
XLA Modules:
  0.0 671.3 jit_solution(12270379611536097252)
XLA Ops:
  5.8 43.5 %all_to_all.183 = f32[2,512,256]{2,0,1:T(2,128)S(1)} all-to-all(f32[2,512,256]{2,0,1:T(2,128)S(1)} %multiply_add_fusion), channel_id=1, replica_groups=mesh['plane'=4,'col'=64] {'col'}, dimensions={1} | all-to-all | bytes 2097152 | tf_op jit(solution)/shard_map/all_to_all | solution.py:66
  49.7 25.2 %slice.127 = f32[2,8,8192]{2,1,0:T(8,128)S(1)} slice(f32[2,8,16388]{2,1,0:T(8,128)S(1)} %pad.33), slice={[0:2:1], [0:8:1], [4:16387:2]} | slice | bytes 1048576 | tf_op jit(solution)/shard_map/slice | solution.py:34
  74.9 25.2 %slice.126 = f32[2,8,8192]{2,1,0:T(8,128)S(1)} slice(f32[2,8,16388]{2,1,0:T(8,128)S(1)} %pad.33), slice={[0:2:1], [0:8:1], [3:16386:2]} | slice | bytes 1048576 | tf_op jit(solution)/shard_map/slice | solution.py:34
  100.1 25.2 %slice.125 = f32[2,8,8192]{2,1,0:T(8,128)S(1)} slice(f32[2,8,16388]{2,1,0:T(8,128)S(1)} %pad.33), slice={[0:2:1], [0:8:1], [2:16385:2]} | slice | bytes 1048576 | tf_op jit(solution)/shard_map/slice | solution.py:34
  125.3 25.2 %slice.124 = f32[2,8,8192]{2,1,0:T(8,128)S(1)} slice(f32[2,8,16388]{2,1,0:T(8,128)S(1)} %pad.33), slice={[0:2:1], [0:8:1], [1:16384:2]} | slice | bytes 1048576 | tf_op jit(solution)/shard_map/slice | solution.py:34
  150.6 25.2 %slice.123 = f32[2,8,8192]{2,1,0:T(8,128)} slice(f32[2,8,16388]{2,1,0:T(8,128)S(1)} %pad.33), slice={[0:2:1], [0:8:1], [0:16383:2]} | slice | bytes 1048576 | tf_op jit(solution)/shard_map/slice | solution.py:32
  184.7 13.0 %reshape.25 = f32[64,1,2048]{2,1,0:T(1,128)S(1)} reshape(f32[8192,2,8]{2,1,0:T(2,128)} %bitcast.115) | data formatting | bytes 1048576
  197.7 25.8 %all_to_all.184 = f32[64,1,2048]{2,1,0:T(1,128)S(1)} all-to-all(f32[64,1,2048]{2,1,0:T(1,128)S(1)} %reshape.25), channel_id=1, replica_groups=mesh['plane'=4,'col'=64] {'col'}, dimensions={0} | all-to-all | bytes 1048576 | tf_op jit(solution)/shard_map/all_to_all | solution.py:72
  226.0 14.0 %reshape.26 = f32[8192,2,8]{2,1,0:T(2,128)} reshape(f32[64,2048]{1,0:T(8,128)S(1)} %reduce.8) | data formatting | bytes 1048576
  250.2 19.3 %all_to_all.185 = f32[2,256,128]{2,0,1:T(2,128)S(1)} all-to-all(f32[2,256,128]{2,0,1:T(2,128)S(1)} %copy.165), channel_id=1, replica_groups=mesh['plane'=4,'col'=64] {'col'}, dimensions={1} | all-to-all | bytes 524288 | tf_op jit(solution)/shard_map/all_to_all | solution.py:66
  304.4 16.9 %all_to_all.186 = f32[64,1,512]{2,1,0:T(1,128)S(1)} all-to-all(f32[64,1,512]{2,1,0:T(1,128)S(1)} %reshape.27), channel_id=1, replica_groups=mesh['plane'=4,'col'=64] {'col'}, dimensions={0} | all-to-all | bytes 262144 | tf_op jit(solution)/shard_map/all_to_all | solution.py:72
  342.6 11.4 %all-to-all-done.7 = f32[64,1,512]{2,1,0:T(1,128)S(1)} async-done(((f32[64,1,512]{2,1,0:T(1,128)}), f32[64,1,512]{2,1,0:T(1,128)S(1)}, u32[]{:S(2)}, u32[]{:S(2)}) %all-to-all-start.7) | async-done | bytes 131104 | tf_op jit(solution)/shard_map/all_to_all | solution.py:66
  368.6 15.4 %copy.215 = f32[2,4,8192]{1,0,2:T(2,128)} copy(f32[2,4,8192]{1,2,0:T(8,128)} %bitcast.117) | data formatting | bytes 524288 | tf_op jit(solution)/shard_map/reshape | solution.py:50
  384.0 14.9 %reshape.31 = f32[64,1,1024]{2,1,0:T(1,128)} reshape(f32[8192,2,4]{2,1,0:T(2,128)} %bitcast.118) | data formatting | bytes 524288
  399.0 12.9 %all-to-all-start.8 = ((f32[64,1,1024]{2,1,0:T(1,128)}), f32[64,1,1024]{2,1,0:T(1,128)S(1)}, u32[]{:S(2)}, u32[]{:S(2)}) async-start(f32[64,1,1024]{2,1,0:T(1,128)} %reshape.31), calls=%async_computation.8 | async-start | bytes 524288 | tf_op jit(solution)/shard_map/all_to_all | solution.py:72
  411.9 13.6 %all-to-all-done.8 = f32[64,1,1024]{2,1,0:T(1,128)S(1)} async-done(((f32[64,1,1024]{2,1,0:T(1,128)}), f32[64,1,1024]{2,1,0:T(1,128)S(1)}, u32[]{:S(2)}, u32[]{:S(2)}) %all-to-all-start.8) | async-done | bytes 262176 | tf_op jit(solution)/shard_map/all_to_all | solution.py:72
  426.8 14.3 %reshape.32 = f32[8192,2,4]{2,1,0:T(2,128)} reshape(f32[64,1024]{1,0:T(8,128)S(1)} %reduce.11) | data formatting | bytes 524288
  469.6 14.7 %copy.155 = f32[2,8,8192,2]{1,3,2,0:T(2,128)} copy(f32[2,8,8192,2]{2,1,0,3:T(8,128)S(1)} %pad_maximum_fusion.1) | data formatting | bytes 2097152 | tf_op jit(solution)/shard_map/stack | solution.py:50
  484.3 28.6 %copy.214 = f32[2,8,16384]{1,0,2:T(2,128)} copy(f32[2,8,16384]{1,2,0:T(8,128)} %bitcast.112) | data formatting | bytes 2097152 | tf_op jit(solution)/shard_map/reshape | solution.py:50
  512.9 29.0 %reshape.33 = f32[64,1,4096]{2,1,0:T(1,128)} reshape(f32[16384,2,8]{2,1,0:T(2,128)} %bitcast.113) | data formatting | bytes 2097152
  547.3 29.1 %all-to-all-done.3 = f32[64,1,4096]{2,1,0:T(1,128)S(1)} async-done(((f32[64,1,4096]{2,1,0:T(1,128)}), f32[64,1,4096]{2,1,0:T(1,128)S(1)}, u32[]{:S(2)}, u32[]{:S(2)}) %all-to-all-start.3) | async-done | bytes 1048608 | tf_op jit(solution)/shard_map/all_to_all | solution.py:72
  579.7 26.7 %reshape.34 = f32[16384,2,8]{2,1,0:T(2,128)} reshape(f32[64,4096]{1,0:T(8,128)S(1)} %reduce.12) | data formatting | bytes 2097152
  606.4 17.6 %copy.185 = f32[2,8,64,256]{3,1,2,0:T(8,128)S(1)} copy(f32[2,8,64,256]{1,0,3,2:T(2,128)} %bitcast.114) | data formatting | bytes 2097152 | tf_op jit(solution)/shard_map/all_to_all | solution.py:72
  639.2 18.2 %collective-permute-done = f32[1,128]{1,0:T(1,128)S(1)} collective-permute-done((f32[1,128]{1,0:T(1,128)S(1)}, f32[1,128]{1,0:T(1,128)S(1)}, u32[]{:S(2)}, u32[]{:S(2)}) %collective-permute-start) | collective-permute-done | bytes 544 | tf_op jit(solution)/shard_map/ppermute | solution.py:17
  (98 shorter events, 165.6 us)
Async XLA Ops:
  336.8 17.3 %all-to-all-start.7 = ((f32[64,1,512]{2,1,0:T(1,128)}), f32[64,1,512]{2,1,0:T(1,128)S(1)}, u32[]{:S(2)}, u32[]{:S(2)}) async-start(f32[64,1,512]{2,1,0:T(1,128)} %reshape.29), calls=%async_computation.7 | async-start | bytes 262144 | tf_op jit(solution)/shard_map/all_to_all | solution.py:66
  354.0 44.9 %all-to-all-start.2 = ((f32[2,512,128]{2,0,1:T(2,128)}), f32[2,512,128]{2,0,1:T(2,128)S(1)}, u32[]{:S(2)}, u32[]{:S(2)}) async-start(f32[2,512,128]{2,0,1:T(2,128)} %copy.153), calls=%async_computation.2 | async-start | bytes 1048576 | tf_op jit(solution)/shard_map/all_to_all | solution.py:66
  399.0 26.6 %all-to-all-start.8 = ((f32[64,1,1024]{2,1,0:T(1,128)}), f32[64,1,1024]{2,1,0:T(1,128)S(1)}, u32[]{:S(2)}, u32[]{:S(2)}) async-start(f32[64,1,1024]{2,1,0:T(1,128)} %reshape.31), calls=%async_computation.8 | async-start | bytes 524288 | tf_op jit(solution)/shard_map/all_to_all | solution.py:72
  452.3 11.9 %all-to-all-start.9 = ((f32[2,512,128]{2,0,1:T(2,128)}), f32[2,512,128]{2,0,1:T(2,128)S(1)}, u32[]{:S(2)}, u32[]{:S(2)}) async-start(f32[2,512,128]{2,0,1:T(2,128)} %copy.176), calls=%async_computation.9 | async-start | bytes 1048576 | tf_op jit(solution)/shard_map/all_to_all | solution.py:87
  458.3 11.2 %copy-start.1 = (f32[2,8,8192,1]{2,1,0,3:T(8,128)S(1)}, f32[2,8,8192,1]{2,1,0,3:T(8,128)}, u32[]{:S(2)}) copy-start(f32[2,8,8192,1]{2,1,0,3:T(8,128)} %get-tuple-element.12) | copy-start | bytes 1572868
  464.2 77.6 %all-to-all-start.10 = ((f32[2,512,128]{2,0,1:T(2,128)}), f32[2,512,128]{2,0,1:T(2,128)S(1)}, u32[]{:S(2)}, u32[]{:S(2)}) async-start(f32[2,512,128]{2,0,1:T(2,128)} %copy.178), calls=%async_computation.10 | async-start | bytes 1048576 | tf_op jit(solution)/shard_map/all_to_all | solution.py:88
  541.8 34.5 %all-to-all-start.3 = ((f32[64,1,4096]{2,1,0:T(1,128)}), f32[64,1,4096]{2,1,0:T(1,128)S(1)}, u32[]{:S(2)}, u32[]{:S(2)}) async-start(f32[64,1,4096]{2,1,0:T(1,128)} %reshape.33), calls=%async_computation.3 | async-start | bytes 2097152 | tf_op jit(solution)/shard_map/all_to_all | solution.py:72
  624.5 1.6 copy-start
  629.8 39.8 %all-to-all-start.4 = ((f32[2,1024,256]{2,0,1:T(2,128)}), f32[2,1024,256]{2,0,1:T(2,128)S(1)}, u32[]{:S(2)}, u32[]{:S(2)}) async-start(f32[2,1024,256]{2,0,1:T(2,128)} %bitcast_subtract_fusion), calls=%async_computation.4 | async-start | bytes 4194304 | tf_op jit(solution)/shard_map/all_to_all | solution.py:86
  633.7 23.8 %collective-permute-start = (f32[1,128]{1,0:T(1,128)S(1)}, f32[1,128]{1,0:T(1,128)S(1)}, u32[]{:S(2)}, u32[]{:S(2)}) collective-permute-start(f32[1,128]{1,0:T(1,128)S(1)} %get-tuple-element.23), channel_id=1, source_target_pairs={{0,64},{64,128},{128,192},{1,65},{65,129},{129,193},{2,66},{66,130... | collective-permute-start | bytes 1544 | tf_op jit(solution)/shard_map/ppermute | solution.py:17
  635.7 21.7 %collective-permute-start.1 = (f32[1,128]{1,0:T(1,128)S(1)}, f32[1,128]{1,0:T(1,128)S(1)}, u32[]{:S(2)}, u32[]{:S(2)}) collective-permute-start(f32[1,128]{1,0:T(1,128)S(1)} %get-tuple-element.24), channel_id=1, source_target_pairs={{64,0},{128,64},{192,128},{65,1},{129,65},{193,129},{66,2},{130,66... | collective-permute-start | bytes 1544 | tf_op jit(solution)/shard_map/ppermute | solution.py:20
  657.5 6.6 collective-permute-start.2
  662.2 6.2 collective-permute-start.3
where the time goes:
time: 680 us; the launch traced here: 671 us
  local copies, waits for them, and re-layouts  410 us (60%)
  blocking collectives  105 us (15%)
  waiting for transfers between devices  81.9 us (12%)
  starting transfers between devices  52.3 us (8%)
  other arithmetic  21.1 us (3%)
    unnamed x15, local copies, waits for them, and re-layouts  131 us
    slice x12, local copies, waits for them, and re-layouts, reduce_along(): lax.slice_in_dim(padded, offset, offset + 2 * amount - 1, 2, along)  120 us
    all_to_all x2, blocking collectives, width_op(): lax.all_to_all(values, 'col', split_axis=1, concat_axis=2, tiled=True)  62.8 us
    reshape x6, local copies, waits for them, and re-layouts, expand_along(): return jnp.stack([even, odd], axis=along + 1).reshape(new_shape)  45.7 us
    all_to_all x8, local copies, waits for them, and re-layouts, width_op(): lax.all_to_all(result, 'col', split_axis=2, concat_axis=1, tiled=True)  43.6 us
    all_to_all x2, blocking collectives, width_op(): lax.all_to_all(result, 'col', split_axis=2, concat_axis=1, tiled=True)  42.7 us
    all_to_all x2, waiting for transfers between devices, width_op(): lax.all_to_all(result, 'col', split_axis=2, concat_axis=1, tiled=True)  42.6 us
    slice x3, local copies, waits for them, and re-layouts, reduce_along(): lax.slice_in_dim(padded, 0, 2 * amount - 1, 2, along)  29.9 us
  transfers between devices with their start and end apart: 11, of which 7 were waited for; matrix products, arithmetic and copies ran while one was open for 18% of the time, Pallas kernels for 0%

commit v1 on v0

v1 whole, which is shorter than its diff:
```python
import functools

import jax
import jax.numpy as jnp
import ml_dtypes
import numpy as np
from jax import lax
from jax.experimental import pallas as pl
from jax.experimental.pallas import tpu as pltpu
from jax.sharding import PartitionSpec as P

TAPS = np.array([1.0, 4.0, 6.0, 4.0, 1.0]) / 16.0
MESH = pl.DeviceIdType.MESH
BF = jnp.bfloat16
F32 = jnp.float32

ROWS = 1024
BLOCK = 256
COLS = 256
WIN = 288
MID = 144
LOW = 80
KEEP = 136
KEEP2 = 72
SUB = 64
SUBS = BLOCK // SUB
EXPO = float(-4.0 * np.log2(np.e))


def reduce_matrix(n):
    m = np.zeros((n // 2, n))
    for i in range(n // 2):
        for t in range(5):
            j = 2 * i - 2 + t
            if 0 <= j < n:
                m[i, j] = TAPS[t]
    return m


def expand_matrix(n):
    m = np.zeros((2 * n, n))
    for j in range(2 * n):
        for i in range(max(0, j // 2 - 2), min(n, j // 2 + 3)):
            t = j - 2 * i + 2
            if 0 <= t <= 4:
                m[j, i] = 2.0 * TAPS[t]
    return m


def window(m, row, rows, col, cols):
    out = np.zeros((rows, cols))
    r0, r1 = max(row, 0), min(row + rows, m.shape[0])
    c0, c1 = max(col, 0), min(col + cols, m.shape[1])
    out[r0 - row : r1 - row, c0 - col : c1 - col] = m[r0:r1, c0:c1]
    return out


def exact(m):
    cast = m.astype(ml_dtypes.bfloat16)
    assert (cast.astype(np.float64) == m).all()
    return cast


@functools.lru_cache(None)
def matrices():
    r0, r1 = reduce_matrix(ROWS), reduce_matrix(ROWS // 2)
    e0 = expand_matrix(ROWS // 2)
    row_in, row_low, row_up = [], [], []
    for p in range(4):
        start = min(max(BLOCK * p - 16, 0), ROWS - WIN)
        m = window(r0, 128 * p - 4, MID, start, WIN)
        row_in.append(np.concatenate([m, m], 1))
        m = window(r1, 64 * p - 2, LOW, 128 * p - 4, MID)
        row_low.append(np.concatenate([m, m], 1))
        m = window(e0, BLOCK * p, BLOCK, 128 * p - 4, MID)
        row_up.append(np.concatenate([m, m], 1))
    m = window(e0, SUB, SUB, 28, 48)
    row_sub = np.concatenate([m, m], 1)
    m = window(expand_matrix(ROWS // 4), 124, MID, 62, LOW)
    row_base = np.concatenate([m, m], 1)
    n = 3 * COLS
    c0, c1 = reduce_matrix(n), reduce_matrix(n // 2)
    x0 = expand_matrix(n // 2)
    col_in, col_halo, col_up = [], [], []
    for b in range(3):
        full = np.concatenate(
            [
                (x0 @ c0)[COLS * b : COLS * (b + 1)],
                c0[128 * b : 128 * (b + 1)],
                window(c1 @ c0, 64 * b - 1, 66, 0, n),
                np.zeros((62, n)),
            ],
            0,
        ).T
        col_in.append(full[COLS * b : COLS * (b + 1)])
        halo = np.zeros((128, 512))
        halo[:16] = window(full, COLS * b - 16, 16, 0, 512)
        halo[16:32] = window(full, COLS * (b + 1), 16, 0, 512)
        col_halo.append(np.concatenate([halo, halo], 0))
        up = x0[COLS * b : COLS * (b + 1)].T
        both = np.zeros((256, COLS))
        both[:128] = up[128 * b : 128 * (b + 1)]
        both[128:129] = window(up, 128 * b - 1, 1, 0, COLS)
        both[129:130] = window(up, 128 * (b + 1), 1, 0, COLS)
        col_up.append(both)
    col_base = np.zeros((128, 128))
    col_base[:66] = window(expand_matrix(n // 4), 128, 128, 63, 66).T
    stacks = (row_in, row_low, row_up, [row_sub], [row_base], col_in, col_halo, col_up, [col_base])
    return tuple(exact(np.stack(s)) for s in stacks)


def split(v):
    hi = v.astype(BF)
    lo = (v - hi.astype(F32)).astype(BF)
    return hi, lo


def dot(a, b):
    return jnp.dot(a, b, preferred_element_type=F32)


def tall(v):
    return jnp.concatenate(split(v), 0)


def inverse(v):
    r = pl.reciprocal(v, approx=True)
    return r * (2.0 - v * r)


def weight(d):
    return jnp.exp2(EXPO * inverse(1.0 + d * d))


def kernel(
    count,
    x_ref, row_in_ref, row_low_ref, row_up_ref, row_sub_ref, row_base_ref,
    col_in_ref, col_halo_ref, col_up_ref, col_base_ref,
    out_ref,
    xwin, m_row_in, m_row_low, m_row_up, m_row_sub, m_row_base, m_col_in, m_col_halo, m_col_up, m_col_base,
    hr, pack, halo, wide, mid, low,
    level0, level1, far0, far1, jbuf, jhalo, upper,
    m_sem, x_sem, swap_send, swap_recv, halo_send, halo_recv, far_send, far_recv, j_send, j_recv,
):
    me = lax.axis_index("plane")
    q = lax.axis_index("col")
    chip, core = me // 2, me % 2
    far = 2 * (1 - chip) + core
    sibling = 2 * chip + 1 - core
    far_sibling = 2 * (1 - chip) + 1 - core
    right = (q + 1) % count
    left = (q + count - 1) % count
    side = (q + count - 2) // (count - 1) + q // (count - 1)
    blocks = (far, me)

    def start_of(p):
        return pl.multiple_of(BLOCK * p - 16 + 16 * ((3 - p) // 3) - 16 * (p // 3), 16)

    def offset_of(p):
        return pl.multiple_of(16 - 16 * ((3 - p) // 3) + 16 * (p // 3), 16)

    own = []
    for b in range(2):
        own.append(
            pltpu.make_async_copy(
                x_ref.at[:, pl.ds(start_of(blocks[b]), WIN)], xwin.at[b, pl.ds(0, 2)], x_sem.at[b]
            )
        )
    loads = [
        (row_in_ref.at[far], m_row_in.at[0]),
        (row_in_ref.at[me], m_row_in.at[1]),
        (col_in_ref.at[side], m_col_in),
        (col_halo_ref.at[side], m_col_halo),
        (row_sub_ref.at[0], m_row_sub),
        (row_low_ref.at[far], m_row_low.at[0]),
        (row_low_ref.at[me], m_row_low.at[1]),
        (col_base_ref.at[0], m_col_base),
        (row_base_ref.at[0], m_row_base),
        (col_up_ref.at[side], m_col_up),
        (row_up_ref.at[me], m_row_up),
    ]
    loads = [pltpu.make_async_copy(s, d, m_sem.at[i]) for i, (s, d) in enumerate(loads)]
    own[0].start()
    loads[0].start()
    own[1].start()
    for copy in loads[1:]:
        copy.start()

    barrier = pltpu.get_barrier_semaphore()
    for plane, col in ((sibling, q), (far, q), (me, left), (me, right)):
        pl.semaphore_signal(barrier, inc=1, device_id=(plane, col), device_id_type=MESH)
    jbuf[pl.ds(KEEP, MID - KEEP)] = jnp.zeros((MID - KEEP, 128), F32)
    pl.semaphore_wait(barrier, 4)

    def remote(src, dst, send, recv, plane, col):
        return pltpu.make_async_remote_copy(
            src_ref=src, dst_ref=dst, send_sem=send, recv_sem=recv, device_id=(plane, col), device_id_type=MESH
        )

    swaps = []
    for b, p in enumerate((far_sibling, sibling)):
        swaps.append(
            remote(
                x_ref.at[:, pl.ds(start_of(p), WIN)],
                xwin.at[b, pl.ds(2, 2)],
                swap_send.at[b],
                swap_recv.at[b],
                sibling,
                q,
            )
        )
    for copy in swaps:
        copy.start()

    lane = lax.broadcasted_iota(jnp.int32, (MID, 128), 1)
    halos = []
    for b in range(2):
        packs = [jnp.zeros((MID, 128), F32), jnp.zeros((MID, 128), F32)]
        for p in range(4):
            if p == 0:
                own[b].wait()
                loads[b].wait()
            if p == 2:
                swaps[b].wait_recv()
            value = dot(m_row_in[b], tall(xwin[b, p]))
            hr[b, p] = value
            here = (lane >= 16 * p) & (lane < 16 * p + 16)
            low_cols = value[:, :128]
            high_cols = value[:, 128:]
            if p > 0:
                low_cols = pltpu.roll(low_cols, 16 * p, 1)
            high_cols = pltpu.roll(high_cols, (16 + 16 * p) % 128, 1)
            packs[0] = jnp.where(here, low_cols, packs[0])
            packs[1] = jnp.where(here, high_cols, packs[1])
        pack[b, 0] = packs[0]
        pack[b, 1] = packs[1]
        for d, col in enumerate((left, right)):
            copy = remote(pack.at[b, d], halo.at[b, 1 - d], halo_send.at[b, d], halo_recv.at[b, 1 - d], me, col)
            copy.start()
            halos.append(copy)

    for copy in loads[2:]:
        copy.wait()

    fars = []

    def send_far(src, dst, i):
        copy = remote(src, dst, far_send.at[i], far_recv.at[i], far, q)
        copy.start()
        fars.append(copy)

    for b in range(2):
        halos[2 * b].wait_recv()
        halos[2 * b + 1].wait_recv()
        for p in range(4):
            hi, lo = split(hr[b, p])
            from_left, from_right = halo[b, 0], halo[b, 1]
            if p > 0:
                from_left = pltpu.roll(from_left, 128 - 16 * p, 1)
            from_right = pltpu.roll(from_right, (128 + 16 - 16 * p) % 128, 1)
            edge = jnp.where(lane < 16, from_left, jnp.where(lane < 32, from_right, 0.0))
            ehi, elo = split(edge)
            value = dot(hi, m_col_in[...]) + dot(lo, m_col_in[...])
            value = value + dot(jnp.concatenate([ehi, elo], 1), m_col_halo[...])
            whi, wlo = split(value[:, :COLS])
            wide[p, 0] = whi
            wide[p, 1] = wlo
            mid[p] = value[:, COLS : COLS + 128]
            low[p] = value[:, COLS + 128 :]

        def join_zero(s):
            num = jnp.zeros((SUB, COLS), F32)
            den = jnp.zeros((SUB, COLS), F32)
            for p in range(4):
                rows = pl.ds(32 * s, 48)
                both = jnp.concatenate([wide[p, 0, rows], wide[p, 1, rows]], 0)
                z = dot(m_row_sub[...], both)
                d = xwin[b, p, pl.ds(pl.multiple_of(offset_of(blocks[b]) + SUB * s, 16), SUB)] - z
                w = weight(d)
                num = num + w * d
                den = den + w
            level0[b, s, 0] = num
            level0[b, s, 1] = den
            if b == 0:
                send_far(level0.at[b, s], far0.at[s], s)

        def join_one():
            num = jnp.zeros((MID, 128), F32)
            den = jnp.zeros((MID, 128), F32)
            total = jnp.zeros((LOW, 128), F32)
            for p in range(4):
                c2 = dot(m_row_low[b], tall(low[p]))
                total = total + c2
                hi, lo = split(c2)
                u = dot(hi, m_col_base[...]) + dot(lo, m_col_base[...])
                base = dot(m_row_base[...], tall(u))
                d = mid[p] - base
                w = weight(d)
                num = num + w * d
                den = den + w
            level1[b, pl.ds(0, KEEP)] = num[:KEEP]
            level1[b, pl.ds(KEEP, KEEP)] = den[:KEEP]
            level1[b, pl.ds(2 * KEEP, KEEP2)] = total[:KEEP2]
            if b == 0:
                send_far(level1.at[b], far1, SUBS)

        join_zero(0)
        join_one()
        for s in range(1, SUBS):
            join_zero(s)

    fars[1].wait_recv()
    num = level1[1, pl.ds(0, KEEP)] + far1[pl.ds(0, KEEP)]
    den = level1[1, pl.ds(KEEP, KEEP)] + far1[pl.ds(KEEP, KEEP)]
    total = level1[1, pl.ds(2 * KEEP, KEEP2)] + far1[pl.ds(2 * KEEP, KEEP2)]
    total = jnp.concatenate([total, jnp.zeros((LOW - KEEP2, 128), F32)], 0)
    hi, lo = split(total)
    u = dot(hi, m_col_base[...]) + dot(lo, m_col_base[...])
    base = dot(m_row_base[...], tall(u))
    jbuf[pl.ds(0, KEEP)] = num * inverse(den) + base[:KEEP] * 0.125
    js = []
    for d, col in enumerate((left, right)):
        copy = remote(jbuf.at[pl.ds(0, KEEP)], jhalo.at[1 - d, pl.ds(0, KEEP)], j_send.at[d], j_recv.at[1 - d], me, col)
        copy.start()
        js.append(copy)
    for copy in js:
        copy.wait_recv()
    from_left = pltpu.roll(jhalo[0, pl.ds(0, KEEP)], 1, 1)
    from_right = pltpu.roll(jhalo[1, pl.ds(0, KEEP)], 1, 1)
    lane = lax.broadcasted_iota(jnp.int32, (KEEP, 128), 1)
    edge = jnp.where(lane == 0, from_left, jnp.where(lane == 1, from_right, 0.0))
    edge = jnp.concatenate([edge, jnp.zeros((MID - KEEP, 128), F32)], 0)
    hi, lo = split(jnp.concatenate([jbuf[...], edge], 1))
    u = dot(hi, m_col_up[...]) + dot(lo, m_col_up[...])
    upper[...] = dot(m_row_up[...], tall(u))

    for s in range(SUBS):
        fars[0 if s == 0 else s + 1].wait_recv()
        num = level0[1, s, 0] + far0[s, 0]
        den = level0[1, s, 1] + far0[s, 1]
        rows = pl.ds(SUB * s, SUB)
        out_ref[rows] = num * inverse(den) + upper[rows]

    for copy in swaps + halos + fars + js:
        copy.wait_send()


def solution(mesh):
    count = mesh.shape["col"]
    consts = matrices()

    def body(x):
        dma = pltpu.SemaphoreType.DMA
        vmem = pltpu.VMEM
        shapes = [c.shape[1:] for c in consts]
        per_block = {0: 2, 1: 2}
        held = [vmem((per_block[i],) + s if i in per_block else s, BF) for i, s in enumerate(shapes)]
        return pl.pallas_call(
            functools.partial(kernel, count),
            out_shape=jax.ShapeDtypeStruct((BLOCK, COLS), F32),
            in_specs=[pl.BlockSpec(memory_space=pl.ANY)] * (1 + len(consts)),
            out_specs=pl.BlockSpec(memory_space=pltpu.VMEM),
            scratch_shapes=[vmem((2, 4, WIN, COLS), F32)]
            + held
            + [
                vmem((2, 4, MID, COLS), F32),
                vmem((2, 2, MID, 128), F32),
                vmem((2, 2, MID, 128), F32),
                vmem((4, 2, MID, COLS), BF),
                vmem((4, MID, 128), F32),
                vmem((4, MID, 128), F32),
                vmem((2, SUBS, 2, SUB, COLS), F32),
                vmem((2, 2 * KEEP + KEEP2, 128), F32),
                vmem((SUBS, 2, SUB, COLS), F32),
                vmem((2 * KEEP + KEEP2, 128), F32),
                vmem((MID, 128), F32),
                vmem((2, MID, 128), F32),
                vmem((BLOCK, COLS), F32),
                dma((11,)),
                dma((2,)),
                dma((2,)),
                dma((2,)),
                dma((2, 2)),
                dma((2, 2)),
                dma((SUBS + 1,)),
                dma((SUBS + 1,)),
                dma((2,)),
                dma((2,)),
            ],
            compiler_params=pltpu.CompilerParams(
                collective_id=0, has_side_effects=True, vmem_limit_bytes=48 * 1024 * 1024
            ),
        )(x, *consts)

    return jax.shard_map(body, mesh=mesh, in_specs=(P("plane", None, "col"),), out_specs=P("plane", "col"), check_vma=False)
```

time: 680 us -> 50.1 us (0.07)
  the two profiles are of different devices: /device:TPU:2 before, /device:TPU:1 now
where the time goes in v1:
time: 50.1 us; the launch traced here: 49.6 us
  Pallas kernels  38.5 us (77%)
  local copies, waits for them, and re-layouts  11.1 us (22%)
    pallas_call x1, Pallas kernels, body(): pl.pallas_call(functools.partial(kernel, count), out_shape=jax.ShapeDtype...  38.5 us
    unnamed x21, local copies, waits for them, and re-layouts  11.1 us

profile of v1, /device:TPU:1, one launch (start us, length us, event | category | flops | bytes accessed | tf_op | source)
XLA Modules:
  0.0 49.6 jit_solution(12332881065135793674)
XLA Ops:
  0.0 0.0 copy-start
  0.0 1.6 %copy-done = f32[2,1024,256]{2,1,0:T(8,128)S(1)} copy-done((f32[2,1024,256]{2,1,0:T(8,128)S(1)}, f32[2,1024,256]{2,1,0:T(8,128)}, u32[]{:S(2)}) %copy-start) | copy-done | bytes 2097176
  1.6 0.0 copy-start.1
  1.6 1.1 %copy-done.1 = bf16[3,256,512]{2,1,0:T(8,128)(2,1)S(1)} copy-done((bf16[3,256,512]{2,1,0:T(8,128)(2,1)S(1)}, bf16[3,256,512]{2,1,0:T(8,128)(2,1)}, u32[]{:S(2)}) %copy-start.1) | copy-done | bytes 786456
  2.7 0.0 copy-start.2
  2.7 1.1 %copy-done.2 = bf16[3,256,512]{2,1,0:T(8,128)(2,1)S(1)} copy-done((bf16[3,256,512]{2,1,0:T(8,128)(2,1)S(1)}, bf16[3,256,512]{2,1,0:T(8,128)(2,1)}, u32[]{:S(2)}) %copy-start.2) | copy-done | bytes 786456
  3.9 0.0 copy-start.3
  3.9 1.1 %copy-done.3 = bf16[4,256,288]{2,1,0:T(8,128)(2,1)S(1)} copy-done((bf16[4,256,288]{2,1,0:T(8,128)(2,1)S(1)}, bf16[4,256,288]{2,1,0:T(8,128)(2,1)}, u32[]{:S(2)}) %copy-start.3) | copy-done | bytes 589848
  5.0 0.0 copy-start.4
  5.0 1.1 %copy-done.4 = bf16[4,144,576]{2,1,0:T(8,128)(2,1)S(1)} copy-done((bf16[4,144,576]{2,1,0:T(8,128)(2,1)S(1)}, bf16[4,144,576]{2,1,0:T(8,128)(2,1)}, u32[]{:S(2)}) %copy-start.4) | copy-done | bytes 663576
  6.1 0.0 copy-start.5
  6.1 1.0 %copy-done.5 = bf16[3,256,256]{2,1,0:T(8,128)(2,1)S(1)} copy-done((bf16[3,256,256]{2,1,0:T(8,128)(2,1)S(1)}, bf16[3,256,256]{2,1,0:T(8,128)(2,1)}, u32[]{:S(2)}) %copy-start.5) | copy-done | bytes 393240
  7.1 0.0 copy-start.6
  7.1 0.9 %copy-done.6 = bf16[4,80,288]{2,1,0:T(8,128)(2,1)S(1)} copy-done((bf16[4,80,288]{2,1,0:T(8,128)(2,1)S(1)}, bf16[4,80,288]{2,1,0:T(8,128)(2,1)}, u32[]{:S(2)}) %copy-start.6) | copy-done | bytes 184344
  8.1 0.0 copy-start.7
  8.1 0.9 %copy-done.7 = bf16[1,144,160]{2,1,0:T(8,128)(2,1)S(1)} copy-done((bf16[1,144,160]{2,1,0:T(8,128)(2,1)S(1)}, bf16[1,144,160]{2,1,0:T(8,128)(2,1)}, u32[]{:S(2)}) %copy-start.7) | copy-done | bytes 46104
  8.9 0.0 copy-start.8
  8.9 0.8 %copy-done.8 = bf16[1,128,128]{2,1,0:T(8,128)(2,1)S(1)} copy-done((bf16[1,128,128]{2,1,0:T(8,128)(2,1)S(1)}, bf16[1,128,128]{2,1,0:T(8,128)(2,1)}, u32[]{:S(2)}) %copy-start.8) | copy-done | bytes 32792
  9.7 0.0 copy-start.9
  9.7 0.7 %copy-done.9 = bf16[1,64,96]{2,1,0:T(8,128)(2,1)S(1)} copy-done((bf16[1,64,96]{2,1,0:T(8,128)(2,1)S(1)}, bf16[1,64,96]{2,1,0:T(8,128)(2,1)}, u32[]{:S(2)}) %copy-start.9) | copy-done | bytes 12312
  10.4 38.5 %shard_map.100 = f32[256,256]{1,0:T(8,128)S(1)} custom-call(f32[2,1024,256]{2,1,0:T(8,128)S(1)} %copy-done, bf16[4,144,576]{2,1,0:T(8,128)(2,1)S(1)} %copy-done.4, bf16[4,80,288]{2,1,0:T(8,128)(2,1)S(1)} %copy-done.6, bf16[4,256,288]{2,1,0:T(8,128)(2,1)S(1)} %copy-done.3, bf16[1,64,96]{2,1,0:T(8,128)(2,1)S(1)} %copy-done.9, ...), custom_call_target="tpu_custom_call" | custom-call | tf_op jit(solution)/shard_map/pallas_call | solution.py:358
  48.9 0.7 %copy.12 = f32[256,256]{1,0:T(8,128)} copy(f32[256,256]{1,0:T(8,128)S(1)} %shard_map.100) | data formatting | bytes 524288
Async XLA Ops:
  0.0 1.6 %copy-start = (f32[2,1024,256]{2,1,0:T(8,128)S(1)}, f32[2,1024,256]{2,1,0:T(8,128)}, u32[]{:S(2)}) copy-start(f32[2,1024,256]{2,1,0:T(8,128)} %x_ref.1) | copy-start | bytes 6291460
  1.6 1.1 %copy-start.1 = (bf16[3,256,512]{2,1,0:T(8,128)(2,1)S(1)}, bf16[3,256,512]{2,1,0:T(8,128)(2,1)}, u32[]{:S(2)}) copy-start(bf16[3,256,512]{2,1,0:T(8,128)(2,1)} %constant.24.clone.col_halo_ref) | copy-start | bytes 2359300
  2.7 1.1 %copy-start.2 = (bf16[3,256,512]{2,1,0:T(8,128)(2,1)S(1)}, bf16[3,256,512]{2,1,0:T(8,128)(2,1)}, u32[]{:S(2)}) copy-start(bf16[3,256,512]{2,1,0:T(8,128)(2,1)} %constant.23.clone.col_in_ref) | copy-start | bytes 2359300
  3.9 1.1 %copy-start.3 = (bf16[4,256,288]{2,1,0:T(8,128)(2,1)S(1)}, bf16[4,256,288]{2,1,0:T(8,128)(2,1)}, u32[]{:S(2)}) copy-start(bf16[4,256,288]{2,1,0:T(8,128)(2,1)} %constant.20.clone.row_up_ref) | copy-start | bytes 1769476
  5.0 1.1 %copy-start.4 = (bf16[4,144,576]{2,1,0:T(8,128)(2,1)S(1)}, bf16[4,144,576]{2,1,0:T(8,128)(2,1)}, u32[]{:S(2)}) copy-start(bf16[4,144,576]{2,1,0:T(8,128)(2,1)} %constant.18.clone.row_in_ref) | copy-start | bytes 1990660
  6.1 1.0 %copy-start.5 = (bf16[3,256,256]{2,1,0:T(8,128)(2,1)S(1)}, bf16[3,256,256]{2,1,0:T(8,128)(2,1)}, u32[]{:S(2)}) copy-start(bf16[3,256,256]{2,1,0:T(8,128)(2,1)} %constant.25.clone.col_up_ref) | copy-start | bytes 1179652
  7.1 0.9 %copy-start.6 = (bf16[4,80,288]{2,1,0:T(8,128)(2,1)S(1)}, bf16[4,80,288]{2,1,0:T(8,128)(2,1)}, u32[]{:S(2)}) copy-start(bf16[4,80,288]{2,1,0:T(8,128)(2,1)} %constant.19.clone.row_low_ref) | copy-start | bytes 552964
  8.1 0.9 %copy-start.7 = (bf16[1,144,160]{2,1,0:T(8,128)(2,1)S(1)}, bf16[1,144,160]{2,1,0:T(8,128)(2,1)}, u32[]{:S(2)}) copy-start(bf16[1,144,160]{2,1,0:T(8,128)(2,1)} %constant.22.clone.row_base_ref) | copy-start | bytes 138244
  8.9 0.8 %copy-start.8 = (bf16[1,128,128]{2,1,0:T(8,128)(2,1)S(1)}, bf16[1,128,128]{2,1,0:T(8,128)(2,1)}, u32[]{:S(2)}) copy-start(bf16[1,128,128]{2,1,0:T(8,128)(2,1)} %constant.26.clone.col_base_ref) | copy-start | bytes 98308
  9.7 0.7 %copy-start.9 = (bf16[1,64,96]{2,1,0:T(8,128)(2,1)S(1)}, bf16[1,64,96]{2,1,0:T(8,128)(2,1)}, u32[]{:S(2)}) copy-start(bf16[1,64,96]{2,1,0:T(8,128)(2,1)} %constant.21.clone.row_sub_ref) | copy-start | bytes 36868

commit v2 on v1

v2 whole, which is shorter than its diff:
```python
import functools

import jax
import jax.numpy as jnp
import ml_dtypes
import numpy as np
from jax import lax
from jax.experimental import pallas as pl
from jax.experimental.pallas import tpu as pltpu
from jax.sharding import PartitionSpec as P

TAPS = np.array([1.0, 4.0, 6.0, 4.0, 1.0]) / 16.0
MESH = pl.DeviceIdType.MESH
BF = jnp.bfloat16
F32 = jnp.float32

ROWS = 1024
BLOCK = 256
COLS = 256
WIN = 288
MID = 144
LOW = 80
KEEP = 136
KEEP2 = 72
SUB = 64
SUBS = BLOCK // SUB
EXT = 67
MESSAGE = 2 * KEEP + KEEP2 + SUB
GATE = 3
EXPO = float(-4.0 * np.log2(np.e))


def reduce_matrix(n):
    m = np.zeros((n // 2, n))
    for i in range(n // 2):
        for t in range(5):
            j = 2 * i - 2 + t
            if 0 <= j < n:
                m[i, j] = TAPS[t]
    return m


def expand_matrix(n):
    m = np.zeros((2 * n, n))
    for j in range(2 * n):
        for i in range(max(0, j // 2 - 2), min(n, j // 2 + 3)):
            t = j - 2 * i + 2
            if 0 <= t <= 4:
                m[j, i] = 2.0 * TAPS[t]
    return m


def window(m, row, rows, col, cols):
    out = np.zeros((rows, cols))
    r0, r1 = max(row, 0), min(row + rows, m.shape[0])
    c0, c1 = max(col, 0), min(col + cols, m.shape[1])
    out[r0 - row : r1 - row, c0 - col : c1 - col] = m[r0:r1, c0:c1]
    return out


def exact(m):
    cast = m.astype(ml_dtypes.bfloat16)
    assert (cast.astype(np.float64) == m).all()
    return cast


@functools.lru_cache(None)
def matrices():
    r0, r1 = reduce_matrix(ROWS), reduce_matrix(ROWS // 2)
    e0 = expand_matrix(ROWS // 2)
    row_in, row_low, row_up = [], [], []
    for p in range(4):
        start = min(max(BLOCK * p - 16, 0), ROWS - WIN)
        m = window(r0, 128 * p - 4, MID, start, WIN)
        row_in.append(np.concatenate([m, m], 1))
        m = window(r1, 64 * p - 2, LOW, 128 * p - 4, MID)
        row_low.append(np.concatenate([m, m], 1))
        m = window(e0, BLOCK * p, BLOCK, 128 * p - 4, MID)
        row_up.append(np.concatenate([m, m], 1))
    m = window(e0, SUB, SUB, 28, 48)
    row_sub = np.concatenate([m, m], 1)
    m = window(expand_matrix(ROWS // 4), 124, MID, 62, LOW)
    row_base = np.concatenate([m, m], 1)
    n = 3 * COLS
    c0, c1 = reduce_matrix(n), reduce_matrix(n // 2)
    x0 = expand_matrix(n // 2)
    col_in, col_halo, col_up = [], [], []
    for b in range(3):
        full = np.concatenate(
            [
                (x0 @ c0)[COLS * b : COLS * (b + 1)],
                c0[128 * b : 128 * (b + 1)],
                window(c1 @ c0, 64 * b - 1, 67, 0, n),
                window(c0, 128 * b - 1, 1, 0, n),
                window(c0, 128 * (b + 1), 1, 0, n),
                np.zeros((59, n)),
            ],
            0,
        ).T
        col_in.append(full[COLS * b : COLS * (b + 1)])
        halo = np.zeros((128, 512))
        halo[:16] = window(full, COLS * b - 16, 16, 0, 512)
        halo[16:32] = window(full, COLS * (b + 1), 16, 0, 512)
        col_halo.append(np.concatenate([halo, halo], 0))
        up = x0[COLS * b : COLS * (b + 1)].T
        both = np.zeros((256, COLS))
        both[:128] = up[128 * b : 128 * (b + 1)]
        both[128 + EXT] = window(up, 128 * b - 1, 1, 0, COLS)[0]
        both[128 + EXT + 1] = window(up, 128 * (b + 1), 1, 0, COLS)[0]
        col_up.append(both)
    col_base = np.zeros((128, 256))
    base = expand_matrix(n // 4)
    col_base[:67, :128] = window(base, 128, 128, 63, 67).T
    col_base[:67, 128 + EXT] = window(base, 127, 1, 63, 67)[0]
    col_base[:67, 128 + EXT + 1] = window(base, 256, 1, 63, 67)[0]
    stacks = (row_in, row_low, row_up, [row_sub], [row_base], col_in, col_halo, col_up, [col_base])
    return tuple(exact(np.stack(s)) for s in stacks)


def split(v):
    hi = v.astype(BF)
    lo = (v - hi.astype(F32)).astype(BF)
    return hi, lo


def dot(a, b):
    return jnp.dot(a, b, preferred_element_type=F32)


def tall(v):
    return jnp.concatenate(split(v), 0)


def inverse(v):
    r = pl.reciprocal(v, approx=True)
    return r * (2.0 - v * r)


def weight(d):
    return jnp.exp2(EXPO * inverse(1.0 + d * d))


def kernel(
    count,
    x_ref, row_in_ref, row_low_ref, row_up_ref, row_sub_ref, row_base_ref,
    col_in_ref, col_halo_ref, col_up_ref, col_base_ref,
    out_ref,
    xwin, m_row_in, m_row_low, m_row_up, m_row_sub, m_row_base, m_col_in, m_col_halo, m_col_up, m_col_base,
    hr, pack, halo, wide, fine,
    level0, level1, far0, far1, jbuf, upper,
    m_sem, x_sem, swap_send, swap_recv, halo_send, halo_recv, far_send, far_recv, group_sem, beside_sem,
):
    me = lax.axis_index("plane")
    q = lax.axis_index("col")
    chip, core = me // 2, me % 2
    far = 2 * (1 - chip) + core
    sibling = 2 * chip + 1 - core
    far_sibling = 2 * (1 - chip) + 1 - core
    side = (q + count - 2) // (count - 1) + q // (count - 1)
    left, right = (q + count - 1) % count, (q + 1) % count
    has_left, has_right = q > 0, q < count - 1
    blocks = (far, me)

    def start_of(p):
        return pl.multiple_of(BLOCK * p - 16 + 16 * ((3 - p) // 3) - 16 * (p // 3), 16)

    def offset_of(p):
        return pl.multiple_of(16 - 16 * ((3 - p) // 3) + 16 * (p // 3), 16)

    own = []
    for b in range(2):
        own.append(
            pltpu.make_async_copy(
                x_ref.at[:, pl.ds(start_of(blocks[b]), WIN)], xwin.at[b, pl.ds(0, 2)], x_sem.at[b]
            )
        )
    loads = [
        (row_in_ref.at[far], m_row_in.at[0]),
        (row_in_ref.at[me], m_row_in.at[1]),
        (col_in_ref.at[side], m_col_in),
        (row_sub_ref.at[0], m_row_sub),
        (col_halo_ref.at[side], m_col_halo),
        (row_low_ref.at[far], m_row_low.at[0]),
        (row_low_ref.at[me], m_row_low.at[1]),
        (col_base_ref.at[0], m_col_base),
        (row_base_ref.at[0], m_row_base),
        (col_up_ref.at[side], m_col_up),
        (row_up_ref.at[me], m_row_up),
    ]
    loads = [pltpu.make_async_copy(s, d, m_sem.at[i]) for i, (s, d) in enumerate(loads)]
    own[0].start()
    loads[0].start()
    loads[2].start()
    loads[3].start()
    own[1].start()
    loads[1].start()
    for copy in loads[4:]:
        copy.start()

    barrier = pltpu.get_barrier_semaphore()

    def tell(sem, plane, col):
        pl.semaphore_signal(sem, inc=1, device_id=(plane, col), device_id_type=MESH)

    @pl.when(sibling != GATE)
    def _():
        tell(barrier, sibling, q)

    @pl.when(far != GATE)
    def _():
        tell(barrier, far, q)

    jbuf[pl.ds(KEEP, MID - KEEP)] = jnp.zeros((MID - KEEP, COLS), F32)

    @pl.when(q == 0)
    def _():
        halo[0] = jnp.zeros((MID, 128), F32)

    @pl.when(q == count - 1)
    def _():
        halo[1] = jnp.zeros((MID, 128), F32)

    @pl.when(me != GATE)
    def _():
        pl.semaphore_wait(barrier, 2)

    @pl.when((sibling == GATE) | (far == GATE))
    def _():
        tell(group_sem, GATE, q)

    @pl.when(me == GATE)
    def _():
        pl.semaphore_wait(group_sem, 2)

        @pl.when(has_left)
        def _():
            tell(barrier, GATE, left)

        @pl.when(has_right)
        def _():
            tell(barrier, GATE, right)

    def remote(src, dst, send, recv, plane, col):
        return pltpu.make_async_remote_copy(
            src_ref=src, dst_ref=dst, send_sem=send, recv_sem=recv, device_id=(plane, col), device_id_type=MESH
        )

    swaps = []
    for b, p in enumerate((far_sibling, sibling)):
        swaps.append(
            remote(
                x_ref.at[:, pl.ds(start_of(p), WIN)],
                xwin.at[b, pl.ds(2, 2)],
                swap_send.at[b],
                swap_recv.at[b],
                sibling,
                q,
            )
        )
    for copy in swaps:
        copy.start()

    lane = lax.broadcasted_iota(jnp.int32, (MID, 128), 1)
    sub_lane = lax.broadcasted_iota(jnp.int32, (SUB, 128), 1)
    low_lane = lax.broadcasted_iota(jnp.int32, (KEEP2, 128), 1)

    def turn(v, by):
        by = by % 128
        return pltpu.roll(v, by, 1) if by else v

    def rows_in(b):
        for p in range(4):
            if p == 0:
                own[b].wait()
                loads[b].wait()
            if p == 2:
                swaps[b].wait_recv()
            hr[b, p] = dot(m_row_in[b], tall(xwin[b, p]))

    def pack_edges(b, packs):
        for p in range(4):
            at = 64 * b + 16 * p
            here = (lane >= at) & (lane < at + 16)
            packs[0] = jnp.where(here, turn(hr[b, p, :, pl.ds(0, 128)], at), packs[0])
            packs[1] = jnp.where(here, turn(hr[b, p, :, pl.ds(128, 128)], 16 + at), packs[1])

    def put_wide(p, value):
        whi, wlo = split(value)
        wide[p, 0] = whi
        wide[p, 1] = wlo

    def sums_zero(b, s):
        num = jnp.zeros((SUB, COLS), F32)
        den = jnp.zeros((SUB, COLS), F32)
        for p in range(4):
            rows = pl.ds(32 * s, 48)
            both = jnp.concatenate([wide[p, 0, rows], wide[p, 1, rows]], 0)
            z = dot(m_row_sub[...], both)
            d = xwin[b, p, pl.ds(pl.multiple_of(offset_of(blocks[b]) + SUB * s, 16), SUB)] - z
            w = weight(d)
            num = num + w * d
            den = den + w
        return num, den

    far_zero = [remote(level0.at[0, s], far0.at[s], far_send.at[s], far_recv.at[s], far, q) for s in range(SUBS)]
    rows_in(0)
    loads[2].wait()
    loads[3].wait()
    for p in range(4):
        hi, lo = split(hr[0, p])
        m = m_col_in[:, pl.ds(0, COLS)]
        put_wide(p, dot(jnp.concatenate([hi, lo], 1), jnp.concatenate([m, m], 0)))
    for s in range(SUBS):
        num, den = sums_zero(0, s)
        level0[0, s, 0] = num
        level0[0, s, 1] = den
        if s < SUBS - 1:
            far_zero[s].start()

    rows_in(1)
    packs = [jnp.zeros((MID, 128), F32), jnp.zeros((MID, 128), F32)]
    pack_edges(0, packs)
    pack_edges(1, packs)
    pack[0] = packs[0]
    pack[1] = packs[1]

    @pl.when(me == GATE)
    def _():
        pl.semaphore_wait(barrier, (q + count - 1) // count + (2 * count - 2 - q) // count)

        for plane in range(GATE):
            tell(beside_sem, plane, q)

    @pl.when(me != GATE)
    def _():
        pl.semaphore_wait(beside_sem, 1)

    to_left = remote(pack.at[0], halo.at[1], halo_send.at[0], halo_recv.at[1], me, left)
    to_right = remote(pack.at[1], halo.at[0], halo_send.at[1], halo_recv.at[0], me, right)

    @pl.when(has_left)
    def _():
        to_left.start()

    @pl.when(has_right)
    def _():
        to_right.start()

    for copy in loads[4:]:
        copy.wait()

    @pl.when(has_left)
    def _():
        to_right.wait_recv()

    @pl.when(has_right)
    def _():
        to_left.wait_recv()

    far_one = remote(level1.at[0], far1, far_send.at[SUBS], far_recv.at[SUBS], far, q)
    for b in range(2):
        for p in range(4):
            hi, lo = split(hr[b, p])
            at = 64 * b + 16 * p
            edge = jnp.where(lane < 16, turn(halo[0], -at), jnp.where(lane < 32, turn(halo[1], 16 - at), 0.0))
            ehi, elo = split(edge)
            m = m_col_in[...]
            value = dot(jnp.concatenate([hi, lo, ehi, elo], 1), jnp.concatenate([m, m, m_col_halo[...]], 0))
            put_wide(p, value[:, :COLS])
            fine[p] = value[:, COLS:]

        num = jnp.zeros((MID, COLS), F32)
        den = jnp.zeros((MID, COLS), F32)
        total = jnp.zeros((LOW, 128), F32)
        for p in range(4):
            c2 = dot(m_row_low[b], tall(fine[p, :, pl.ds(128, 128)]))
            total = total + c2
            hi, lo = split(c2)
            m = m_col_base[...]
            u = dot(jnp.concatenate([hi, lo], 1), jnp.concatenate([m, m], 0))
            d = fine[p] - dot(m_row_base[...], tall(u))
            w = weight(d)
            num = num + w * d
            den = den + w
        level1[b, pl.ds(0, KEEP)] = num[:KEEP, :128]
        level1[b, pl.ds(KEEP, KEEP)] = den[:KEEP, :128]
        tile = turn(den[64 : 64 + KEEP2, 128:], 6)
        tile = jnp.where(low_lane < EXT + 6, turn(den[:KEEP2, 128:], 4), tile)
        tile = jnp.where(low_lane < EXT + 4, turn(num[64 : 64 + KEEP2, 128:], 2), tile)
        tile = jnp.where(low_lane < EXT + 2, num[:KEEP2, 128:], tile)
        level1[b, pl.ds(2 * KEEP, KEEP2)] = jnp.where(low_lane < EXT, total[:KEEP2], tile)

        patch = jnp.zeros((SUB, 128), F32)
        for s in range(SUBS):
            num, den = sums_zero(b, s)
            if b == 0:
                for at, v in ((8 * s, num), (32 + 8 * s, den)):
                    edges = jnp.where(sub_lane < 64, v[:, :128], v[:, 128:])
                    patch = jnp.where((sub_lane >= at) & (sub_lane < at + 8), turn(edges, 4 + at), patch)
            else:
                level0[1, s, 0] = num
                level0[1, s, 1] = den
        if b == 0:
            level1[0, pl.ds(2 * KEEP + KEEP2, SUB)] = patch
            far_one.start()
            far_zero[SUBS - 1].start()

    far_one.wait_recv()
    rows = pl.ds(2 * KEEP, KEEP2)
    tile = level1[1, rows] + far1[rows]
    total = jnp.concatenate([jnp.where(low_lane < EXT, tile, 0.0), jnp.zeros((LOW - KEEP2, 128), F32)], 0)
    hi, lo = split(total)
    m = m_col_base[...]
    u = dot(jnp.concatenate([hi, lo], 1), jnp.concatenate([m, m], 0))
    base = dot(m_row_base[...], tall(u))
    num = level1[1, pl.ds(0, KEEP)] + far1[pl.ds(0, KEEP)]
    den = level1[1, pl.ds(KEEP, KEEP)] + far1[pl.ds(KEEP, KEEP)]
    jbuf[pl.ds(0, KEEP), pl.ds(0, 128)] = num * inverse(den) + base[:KEEP, :128] * 0.125
    outer = (low_lane >= EXT) & (low_lane < EXT + 4)
    ratio = jnp.where(outer, tile, 0.0) * inverse(jnp.where(outer, turn(tile, -4), 1.0))
    ratio = jnp.concatenate([ratio[:64], turn(ratio, -2)], 0) + base[:KEEP, 128:] * 0.125
    keep_lane = lax.broadcasted_iota(jnp.int32, (KEEP, 128), 1)
    ratio = jnp.where((keep_lane >= EXT) & (keep_lane < EXT + 2), ratio, 0.0)
    jbuf[pl.ds(0, KEEP), pl.ds(128, 128)] = ratio
    hi, lo = split(jbuf[...])
    m = m_col_up[...]
    u = dot(jnp.concatenate([hi, lo], 1), jnp.concatenate([m, m], 0))
    upper[...] = dot(m_row_up[...], tall(u))

    patch = far1[pl.ds(2 * KEEP + KEEP2, SUB)]
    for s in range(SUBS):
        far_zero[s].wait_recv()
        sums = []
        for i in range(2):
            edges = turn(patch, -(4 + 32 * i + 8 * s))
            first = jnp.where(sub_lane < 4, edges, far0[s, i, :, pl.ds(0, 128)])
            second = jnp.where(sub_lane >= 124, edges, far0[s, i, :, pl.ds(128, 128)])
            sums.append(level0[1, s, i] + jnp.concatenate([first, second], 1))
        rows = pl.ds(SUB * s, SUB)
        out_ref[rows] = sums[0] * inverse(sums[1]) + upper[rows]

    @pl.when(has_left)
    def _():
        to_left.wait_send()

    @pl.when(has_right)
    def _():
        to_right.wait_send()

    for copy in swaps + far_zero + [far_one]:
        copy.wait_send()


def solution(mesh):
    count = mesh.shape["col"]
    consts = matrices()

    def body(x):
        dma = pltpu.SemaphoreType.DMA
        vmem = pltpu.VMEM
        shapes = [c.shape[1:] for c in consts]
        per_block = {0: 2, 1: 2}
        held = [vmem((per_block[i],) + s if i in per_block else s, BF) for i, s in enumerate(shapes)]
        return pl.pallas_call(
            functools.partial(kernel, count),
            out_shape=jax.ShapeDtypeStruct((BLOCK, COLS), F32),
            in_specs=[pl.BlockSpec(memory_space=pl.ANY)] * (1 + len(consts)),
            out_specs=pl.BlockSpec(memory_space=pltpu.VMEM),
            scratch_shapes=[vmem((2, 4, WIN, COLS), F32)]
            + held
            + [
                vmem((2, 4, MID, COLS), F32),
                vmem((2, MID, 128), F32),
                vmem((2, MID, 128), F32),
                vmem((4, 2, MID, COLS), BF),
                vmem((4, MID, COLS), F32),
                vmem((2, SUBS, 2, SUB, COLS), F32),
                vmem((2, MESSAGE, 128), F32),
                vmem((SUBS, 2, SUB, COLS), F32),
                vmem((MESSAGE, 128), F32),
                vmem((MID, COLS), F32),
                vmem((BLOCK, COLS), F32),
                dma((11,)),
                dma((2,)),
                dma((2,)),
                dma((2,)),
                dma((2,)),
                dma((2,)),
                dma((SUBS + 1,)),
                dma((SUBS + 1,)),
                pltpu.SemaphoreType.REGULAR,
                pltpu.SemaphoreType.REGULAR,
            ],
            compiler_params=pltpu.CompilerParams(
                collective_id=0, has_side_effects=True, vmem_limit_bytes=63 * 1024 * 1024
            ),
        )(x, *consts)

    return jax.shard_map(body, mesh=mesh, in_specs=(P("plane", None, "col"),), out_specs=P("plane", "col"), check_vma=False)
```

time: 50.1 us -> 30.9 us (0.62)
  the two profiles are of different devices: /device:TPU:1 before, /device:TPU:6 now
where the time goes in v2:
time: 30.9 us; the launch traced here: 30.7 us
  Pallas kernels  29 us (94%)
  local copies, waits for them, and re-layouts  1.67 us (5%)
    pallas_call x1, Pallas kernels, body(): pl.pallas_call(functools.partial(kernel, count), out_shape=jax.ShapeDtype...  29 us
    unnamed x1, local copies, waits for them, and re-layouts  1.67 us

profile of v2, /device:TPU:6, one launch (start us, length us, event | category | flops | bytes accessed | tf_op | source)
XLA Modules:
  0.0 30.7 jit_solution(3299547476777334541)
XLA Ops:
  0.0 29.0 %shard_map.100 = f32[256,256]{1,0:T(8,128)} custom-call(f32[2,1024,256]{2,1,0:T(8,128)} %x_ref.1, bf16[4,144,576]{2,1,0:T(8,128)(2,1)} %constant.18.clone.row_in_ref, bf16[4,80,288]{2,1,0:T(8,128)(2,1)} %constant.19.clone.row_low_ref, bf16[4,256,288]{2,1,0:T(8,128)(2,1)} %constant.20.clone.row_up_ref, bf16[1,64,96]{2,1,0:T(8,128)(2,1)} %constant.21.clone.row_sub_ref, ...), custom_call_target="tpu_custom_call" | custom-call | tf_op jit(solution)/shard_map/pallas_call | solution.py:464
  29.1 1.7 %copy.12 = f32[256,256]{1,0:T(8,128)} copy(f32[256,256]{1,0:T(8,128)} %shard_map.100) | data formatting | bytes 524288

commit v3 on v2

v3 whole, which is shorter than its diff:
```python
import functools

import jax
import jax.numpy as jnp
import ml_dtypes
import numpy as np
from jax import lax
from jax.experimental import pallas as pl
from jax.experimental.pallas import tpu as pltpu
from jax.sharding import PartitionSpec as P

TAPS = np.array([1.0, 4.0, 6.0, 4.0, 1.0]) / 16.0
MESH = pl.DeviceIdType.MESH
BF = jnp.bfloat16
F32 = jnp.float32

ROWS = 1024
BLOCK = 256
COLS = 256
WIN = 288
MID = 144
LOW = 80
KEEP = 136
KEEP2 = 72
SUB = 64
SUBS = BLOCK // SUB
EXT = 67
WIDE = 640
ROW_PART = MID + LOW + BLOCK
COL_PART = 3 * 256
REST = 4 * ROW_PART + 3 * COL_PART
LATE = KEEP2 + SUB // 2
EDGE = 76
VMEM_BYTES = 52 * 1024 * 1024
GATE = 3
EXPO = float(-4.0 * np.log2(np.e))


def reduce_matrix(n):
    m = np.zeros((n // 2, n))
    for i in range(n // 2):
        for t in range(5):
            j = 2 * i - 2 + t
            if 0 <= j < n:
                m[i, j] = TAPS[t]
    return m


def expand_matrix(n):
    m = np.zeros((2 * n, n))
    for j in range(2 * n):
        for i in range(max(0, j // 2 - 2), min(n, j // 2 + 3)):
            t = j - 2 * i + 2
            if 0 <= t <= 4:
                m[j, i] = 2.0 * TAPS[t]
    return m


def window(m, row, rows, col, cols):
    out = np.zeros((rows, cols))
    r0, r1 = max(row, 0), min(row + rows, m.shape[0])
    c0, c1 = max(col, 0), min(col + cols, m.shape[1])
    out[r0 - row : r1 - row, c0 - col : c1 - col] = m[r0:r1, c0:c1]
    return out


def exact(m):
    cast = m.astype(ml_dtypes.bfloat16)
    assert (cast.astype(np.float64) == m).all()
    return cast


@functools.lru_cache(None)
def matrices():
    r0, r1 = reduce_matrix(ROWS), reduce_matrix(ROWS // 2)
    e0 = expand_matrix(ROWS // 2)
    row_in, row_low, row_up = [], [], []
    for p in range(4):
        start = min(max(BLOCK * p - 16, 0), ROWS - WIN)
        m = window(r0, 128 * p - 4, MID, start, WIN)
        row_in.append(np.concatenate([m, m], 1))
        m = window(r1, 64 * p - 2, LOW, 128 * p - 4, MID)
        row_low.append(np.concatenate([m, m], 1))
        m = window(e0, BLOCK * p, BLOCK, 128 * p - 4, MID)
        row_up.append(np.concatenate([m, m], 1))
    m = window(e0, SUB, SUB, 28, 48)
    row_sub = np.concatenate([m, m], 1)
    m = window(expand_matrix(ROWS // 4), 124, MID, 62, LOW)
    row_base = np.concatenate([m, m], 1)
    n = 3 * COLS
    c0, c1 = reduce_matrix(n), reduce_matrix(n // 2)
    x0 = expand_matrix(n // 2)
    col_in, col_halo, col_up = [], [], []
    for b in range(3):
        full = np.concatenate(
            [
                (x0 @ c0)[COLS * b : COLS * (b + 1)],
                c0[128 * b : 128 * (b + 1)],
                window(c1 @ c0, 64 * b - 1, 67, 0, n),
                window(c0, 128 * b - 1, 1, 0, n),
                window(c0, 128 * (b + 1), 1, 0, n),
                np.zeros((59, n)),
            ],
            0,
        ).T
        col_in.append(full[COLS * b : COLS * (b + 1)])
        halo = np.zeros((128, 512))
        halo[:16] = window(full, COLS * b - 16, 16, 0, 512)
        halo[16:32] = window(full, COLS * (b + 1), 16, 0, 512)
        col_halo.append(np.concatenate([halo, halo], 0))
        up = x0[COLS * b : COLS * (b + 1)].T
        both = np.zeros((256, COLS))
        both[:128] = up[128 * b : 128 * (b + 1)]
        both[128 + EXT] = window(up, 128 * b - 1, 1, 0, COLS)[0]
        both[128 + EXT + 1] = window(up, 128 * (b + 1), 1, 0, COLS)[0]
        col_up.append(both)
    col_base = np.zeros((128, 256))
    base = expand_matrix(n // 4)
    col_base[:67, :128] = window(base, 128, 128, 63, 67).T
    col_base[:67, 128 + EXT] = window(base, 127, 1, 63, 67)[0]
    col_base[:67, 128 + EXT + 1] = window(base, 256, 1, 63, 67)[0]
    parts = []
    for p in range(4):
        parts += [row_in[p], row_low[p], row_up[p]]
    for b in range(3):
        parts += [col_in[b], col_halo[b], col_up[b]]
    parts += [col_base, row_base, row_sub]
    return np.concatenate([exact(np.pad(m, ((0, 0), (0, WIDE - m.shape[1])))) for m in parts], 0)


def split(v):
    hi = v.astype(BF)
    lo = (v - hi.astype(F32)).astype(BF)
    return hi, lo


def dot(a, b):
    return jnp.dot(a, b, preferred_element_type=F32)


def tall(v):
    return jnp.concatenate(split(v), 0)


def inverse(v):
    r = pl.reciprocal(v, approx=True)
    return r * (2.0 - v * r)


def weight(d):
    return jnp.exp2(EXPO * inverse(1.0 + d * d))


def kernel(
    count,
    x_ref, const_ref,
    out_ref,
    xwin, m_row_in, m_row_low, m_row_up, m_row_sub, m_row_base, m_col_in, m_col_halo, m_col_up, m_col_base,
    hr, pack, halo, wide, c1, low,
    level0, level1, late, far0, far1, far_late, jbuf, upper,
    m_sem, x_sem, swap_send, swap_recv, halo_send, halo_recv, far_send, far_recv, group_sem, beside_sem,
):
    me = lax.axis_index("plane")
    q = lax.axis_index("col")
    chip, core = me // 2, me % 2
    far = 2 * (1 - chip) + core
    sibling = 2 * chip + 1 - core
    far_sibling = 2 * (1 - chip) + 1 - core
    side = (q + count - 2) // (count - 1) + q // (count - 1)
    left, right = (q + count - 1) % count, (q + 1) % count
    has_left, has_right = q > 0, q < count - 1
    blocks = (far, me)

    def start_of(p):
        return pl.multiple_of(BLOCK * p - 16 + 16 * ((3 - p) // 3) - 16 * (p // 3), 16)

    def offset_of(p):
        return pl.multiple_of(16 - 16 * ((3 - p) // 3) + 16 * (p // 3), 16)

    own = []
    for b in range(2):
        own.append(
            pltpu.make_async_copy(
                x_ref.at[:, pl.ds(start_of(blocks[b]), WIN)], xwin.at[b, pl.ds(0, 2)], x_sem.at[b]
            )
        )

    def const(at, rows, cols):
        return const_ref.at[pl.ds(pl.multiple_of(at, 16), rows), pl.ds(0, cols)]

    col_at = 4 * ROW_PART + COL_PART * side
    loads = [
        (const(ROW_PART * far, MID, WIDE), m_row_in.at[0]),
        (const(ROW_PART * me, MID, WIDE), m_row_in.at[1]),
        (const(col_at, 256, 512), m_col_in),
        (const(REST + 128 + MID, SUB, 128), m_row_sub),
        (const(ROW_PART * far + MID, LOW, 384), m_row_low.at[0]),
        (const(REST, 128, 256), m_col_base),
        (const(REST + 128, MID, 256), m_row_base),
        (const(col_at + 256, 256, 512), m_col_halo),
        (const(ROW_PART * me + MID, LOW, 384), m_row_low.at[1]),
        (const(col_at + 512, 256, 256), m_col_up),
        (const(ROW_PART * me + MID + LOW, BLOCK, 384), m_row_up),
    ]
    loads = [pltpu.make_async_copy(s, d, m_sem.at[i]) for i, (s, d) in enumerate(loads)]
    own[0].start()
    loads[0].start()
    loads[2].start()
    loads[3].start()

    barrier = pltpu.get_barrier_semaphore()

    def tell(sem, plane, col):
        pl.semaphore_signal(sem, inc=1, device_id=(plane, col), device_id_type=MESH)

    @pl.when(sibling != GATE)
    def _():
        tell(barrier, sibling, q)

    @pl.when(far != GATE)
    def _():
        tell(barrier, far, q)

    own[1].start()
    loads[1].start()
    for copy in loads[4:]:
        copy.start()
    jbuf[pl.ds(KEEP, MID - KEEP)] = jnp.zeros((MID - KEEP, COLS), F32)

    @pl.when(q == 0)
    def _():
        halo[0] = jnp.zeros((MID, 128), F32)

    @pl.when(q == count - 1)
    def _():
        halo[1] = jnp.zeros((MID, 128), F32)

    @pl.when(me != GATE)
    def _():
        pl.semaphore_wait(barrier, 2)

    @pl.when((sibling == GATE) | (far == GATE))
    def _():
        tell(group_sem, GATE, q)

    @pl.when(me == GATE)
    def _():
        pl.semaphore_wait(group_sem, 2)

        @pl.when(has_left)
        def _():
            tell(barrier, GATE, left)

        @pl.when(has_right)
        def _():
            tell(barrier, GATE, right)

    def remote(src, dst, send, recv, plane, col):
        return pltpu.make_async_remote_copy(
            src_ref=src, dst_ref=dst, send_sem=send, recv_sem=recv, device_id=(plane, col), device_id_type=MESH
        )

    swaps = []
    for b, p in enumerate((far_sibling, sibling)):
        swaps.append(
            remote(
                x_ref.at[:, pl.ds(start_of(p), WIN)],
                xwin.at[b, pl.ds(2, 2)],
                swap_send.at[b],
                swap_recv.at[b],
                sibling,
                q,
            )
        )
    for copy in swaps:
        copy.start()

    lane = lax.broadcasted_iota(jnp.int32, (MID, 128), 1)
    half_lane = lax.broadcasted_iota(jnp.int32, (SUB // 2, 128), 1)
    sub_lane = lax.broadcasted_iota(jnp.int32, (SUB, 128), 1)
    low_lane = lax.broadcasted_iota(jnp.int32, (KEEP2, 128), 1)
    keep_lane = lax.broadcasted_iota(jnp.int32, (KEEP, 128), 1)

    def turn(v, by):
        by = by % 128
        return pltpu.roll(v, by, 1) if by else v

    def rows_in(b, p):
        if p == 0:
            own[b].wait()
            loads[b].wait()
        if p == 2:
            swaps[b].wait_recv()
        value = dot(m_row_in[b, :, pl.ds(0, 2 * WIN)], tall(xwin[b, p]))
        hr[b, p] = value
        return value

    def put(p, value):
        whi, wlo = split(value[:, :COLS])
        wide[p, 0] = whi
        wide[p, 1] = wlo
        c1[p] = value[:, COLS : COLS + 128]
        low[:, pl.ds(128 * p, 128)] = value[:, COLS + 128 :]

    def sums_zero(b, s):
        num = jnp.zeros((SUB, COLS), F32)
        den = jnp.zeros((SUB, COLS), F32)
        for p in range(4):
            rows = pl.ds(32 * s, 48)
            both = jnp.concatenate([wide[p, 0, rows], wide[p, 1, rows]], 0)
            z = dot(m_row_sub[:, pl.ds(0, 96)], both)
            d = xwin[b, p, pl.ds(pl.multiple_of(offset_of(blocks[b]) + SUB * s, 16), SUB)] - z
            w = weight(d)
            num = num + w * d
            den = den + w
        return num, den

    def twice(ref):
        m = ref[...]
        return jnp.concatenate([m, m], 0)

    def columns_up(c2):
        return dot(jnp.concatenate(split(c2), 1), twice(m_col_base))

    def sums_one(b):
        c2 = dot(m_row_low[b, :, pl.ds(0, 2 * MID)], tall(low[...]))
        parts = [c2[:, 128 * p : 128 * p + 128] for p in range(4)]
        u = columns_up(jnp.concatenate(parts, 0))
        u = jnp.concatenate([u[LOW * p : LOW * p + LOW] for p in range(4)], 1)
        base = dot(m_row_base[:, pl.ds(0, 2 * LOW)], tall(u))
        num = jnp.zeros((MID, COLS), F32)
        den = jnp.zeros((MID, COLS), F32)
        for p in range(4):
            d = jnp.concatenate([c1[p], low[:, pl.ds(128 * p, 128)]], 1) - base[:, COLS * p : COLS * p + COLS]
            w = weight(d)
            num = num + w * d
            den = den + w
        return num, den, parts[0] + parts[1] + parts[2] + parts[3]

    def put_one(b, num, den):
        level1[b, 0] = num[:KEEP, :128]
        level1[b, 1] = den[:KEEP, :128]

    def late_tile(num, den, total):
        tile = turn(den[64 : 64 + KEEP2, 128:], 6)
        tile = jnp.where(low_lane < EXT + 6, turn(den[:KEEP2, 128:], 4), tile)
        tile = jnp.where(low_lane < EXT + 4, turn(num[64 : 64 + KEEP2, 128:], 2), tile)
        tile = jnp.where(low_lane < EXT + 2, num[:KEEP2, 128:], tile)
        tile = jnp.where(low_lane < EXT, total[:KEEP2], tile)
        for i, v in enumerate((num, den)):
            for h in range(2):
                at = EDGE + 20 * i + 10 * h
                tile = jnp.where(low_lane >= at, turn(v[64 * h : 64 * h + KEEP2, :128], 4 + at), tile)
        return tile

    far_zero = [remote(level0.at[0, s], far0.at[s], far_send.at[s], far_recv.at[s], far, q) for s in range(SUBS)]
    far_one = remote(level1.at[0], far1, far_send.at[SUBS], far_recv.at[SUBS], far, q)
    far_last = remote(late.at[0], far_late, far_send.at[SUBS + 1], far_recv.at[SUBS + 1], far, q)
    for p in range(4):
        value = rows_in(0, p)
        if p == 0:
            loads[2].wait()
            loads[3].wait()
        put(p, dot(jnp.concatenate(split(value), 1), twice(m_col_in)))

    def far_chunk(s):
        num, den = sums_zero(0, s)
        level0[0, s, 0] = num
        level0[0, s, 1] = den
        if s < SUBS - 1:
            far_zero[s].start()

    far_chunk(0)
    for p in range(4):
        rows_in(1, p)
    packs = [jnp.zeros((MID, 128), F32), jnp.zeros((MID, 128), F32)]
    for b in range(2):
        for p in range(4):
            at = 64 * b + 16 * p
            here = (lane >= at) & (lane < at + 16)
            packs[0] = jnp.where(here, turn(hr[b, p, :, pl.ds(0, 128)], at), packs[0])
            packs[1] = jnp.where(here, turn(hr[b, p, :, pl.ds(128, 128)], 16 + at), packs[1])
    pack[0] = packs[0]
    pack[1] = packs[1]

    to_left = remote(pack.at[0], halo.at[1], halo_send.at[0], halo_recv.at[1], me, left)
    to_right = remote(pack.at[1], halo.at[0], halo_send.at[1], halo_recv.at[0], me, right)

    def send_halo():
        @pl.when(me == GATE)
        def _():
            pl.semaphore_wait(barrier, (q + count - 1) // count + (2 * count - 2 - q) // count)
            for plane in range(GATE):
                tell(beside_sem, plane, q)

        @pl.when(me != GATE)
        def _():
            pl.semaphore_wait(beside_sem, 1)

        @pl.when(has_left)
        def _():
            to_left.start()

        @pl.when(has_right)
        def _():
            to_right.start()

    ahead = q % 8 == 0
    pl.when(jnp.logical_not(ahead))(send_halo)

    for s in range(1, SUBS):
        far_chunk(s)
    for copy in loads[4:7]:
        copy.wait()
    num, den, _ = sums_one(0)
    put_one(0, num, den)
    far_one.start()

    pl.when(ahead)(send_halo)

    for copy in loads[7:]:
        copy.wait()

    @pl.when(has_left)
    def _():
        to_right.wait_recv()

    @pl.when(has_right)
    def _():
        to_left.wait_recv()

    for b in range(2):
        for p in range(4):
            at = 64 * b + 16 * p
            edge = jnp.where(lane < 16, turn(halo[0], -at), jnp.where(lane < 32, turn(halo[1], 16 - at), 0.0))
            lhs = jnp.concatenate(split(hr[b, p]) + split(edge), 1)
            put(p, dot(lhs, jnp.concatenate([twice(m_col_in), m_col_halo[...]], 0)))

        num, den, total = sums_one(b)
        late[b, pl.ds(0, KEEP2)] = late_tile(num, den, total)
        if b == 1:
            put_one(b, num, den)

        patch = jnp.zeros((SUB // 2, 128), F32)
        for s in range(SUBS):
            num, den = sums_zero(b, s)
            if b == 1:
                level0[1, s, 0] = num
                level0[1, s, 1] = den
                continue
            for i, v in enumerate((num, den)):
                edges = jnp.where(sub_lane < 64, v[:, :128], v[:, 128:])
                for h in range(2):
                    at = 32 * s + 16 * h + 8 * i
                    moved = turn(edges[32 * h : 32 * h + 32], 4 + at)
                    patch = jnp.where((half_lane >= at) & (half_lane < at + 8), moved, patch)
        if b == 0:
            late[0, pl.ds(KEEP2, SUB // 2)] = patch
            far_last.start()
            far_zero[SUBS - 1].start()

    far_one.wait_recv()
    far_last.wait_recv()
    own_tile, far_tile = late[1, pl.ds(0, KEEP2)], far_late[pl.ds(0, KEEP2)]
    tile = own_tile + far_tile
    total = jnp.concatenate([jnp.where(low_lane < EXT, tile, 0.0), jnp.zeros((LOW - KEEP2, 128), F32)], 0)
    base = dot(m_row_base[:, pl.ds(0, 2 * LOW)], tall(columns_up(total)))
    at_edge = (keep_lane < 6) | (keep_lane >= 124)
    sums = []
    for i in range(2):
        at = EDGE + 20 * i
        edges = jnp.concatenate([turn(far_tile, -(4 + at))[:64], turn(far_tile, -(14 + at))], 0)
        sums.append(level1[1, i] + jnp.where(at_edge, edges, far1[i]))
    jbuf[pl.ds(0, KEEP), pl.ds(0, 128)] = sums[0] * inverse(sums[1]) + base[:KEEP, :128] * 0.125
    outer = (low_lane >= EXT) & (low_lane < EXT + 4)
    ratio = jnp.where(outer, tile, 0.0) * inverse(jnp.where(outer, turn(tile, -4), 1.0))
    ratio = jnp.concatenate([ratio[:64], turn(ratio, -2)], 0) + base[:KEEP, 128:] * 0.125
    ratio = jnp.where((keep_lane >= EXT) & (keep_lane < EXT + 2), ratio, 0.0)
    jbuf[pl.ds(0, KEEP), pl.ds(128, 128)] = ratio
    u = dot(jnp.concatenate(split(jbuf[...]), 1), twice(m_col_up))
    upper[...] = dot(m_row_up[:, pl.ds(0, 2 * MID)], tall(u))

    patch = far_late[pl.ds(KEEP2, SUB // 2)]
    for s in range(SUBS):
        far_zero[s].wait_recv()
        sums = []
        for i in range(2):
            at = 32 * s + 8 * i
            edges = jnp.concatenate([turn(patch, -(4 + at)), turn(patch, -(20 + at))], 0)
            first = jnp.where(sub_lane < 4, edges, far0[s, i, :, pl.ds(0, 128)])
            second = jnp.where(sub_lane >= 124, edges, far0[s, i, :, pl.ds(128, 128)])
            sums.append(level0[1, s, i] + jnp.concatenate([first, second], 1))
        rows = pl.ds(SUB * s, SUB)
        out_ref[rows] = sums[0] * inverse(sums[1]) + upper[rows]

    @pl.when(has_left)
    def _():
        to_left.wait_send()

    @pl.when(has_right)
    def _():
        to_right.wait_send()

    for copy in swaps + far_zero + [far_one, far_last]:
        copy.wait_send()


def solution(mesh):
    count = mesh.shape["col"]
    consts = matrices()

    def body(x):
        dma = pltpu.SemaphoreType.DMA
        vmem = pltpu.VMEM
        return pl.pallas_call(
            functools.partial(kernel, count),
            out_shape=jax.ShapeDtypeStruct((BLOCK, COLS), F32),
            in_specs=[pl.BlockSpec(memory_space=pl.ANY)] * 2,
            out_specs=pl.BlockSpec(memory_space=pltpu.VMEM),
            scratch_shapes=[
                vmem((2, 4, WIN, COLS), F32),
                vmem((2, MID, WIDE), BF),
                vmem((2, LOW, 384), BF),
                vmem((BLOCK, 384), BF),
                vmem((SUB, 128), BF),
                vmem((MID, 256), BF),
                vmem((256, 512), BF),
                vmem((256, 512), BF),
                vmem((256, 256), BF),
                vmem((128, 256), BF),
                vmem((2, 4, MID, COLS), F32),
                vmem((2, MID, 128), F32),
                vmem((2, MID, 128), F32),
                vmem((4, 2, MID, COLS), BF),
                vmem((4, MID, 128), F32),
                vmem((MID, 512), F32),
                vmem((2, SUBS, 2, SUB, COLS), F32),
                vmem((2, 2, KEEP, 128), F32),
                vmem((2, LATE, 128), F32),
                vmem((SUBS, 2, SUB, COLS), F32),
                vmem((2, KEEP, 128), F32),
                vmem((LATE, 128), F32),
                vmem((MID, COLS), F32),
                vmem((BLOCK, COLS), F32),
                dma((11,)),
                dma((2,)),
                dma((2,)),
                dma((2,)),
                dma((2,)),
                dma((2,)),
                dma((SUBS + 2,)),
                dma((SUBS + 2,)),
                pltpu.SemaphoreType.REGULAR,
                pltpu.SemaphoreType.REGULAR,
            ],
            compiler_params=pltpu.CompilerParams(
                collective_id=0, has_side_effects=True, vmem_limit_bytes=VMEM_BYTES
            ),
        )(x, consts)

    return jax.shard_map(body, mesh=mesh, in_specs=(P("plane", None, "col"),), out_specs=P("plane", "col"), check_vma=False)
```

time: 30.9 us -> 24.8 us (0.80)
  the two profiles are of different devices: /device:TPU:6 before, /device:TPU:1 now
where the time goes in v3:
time: 24.8 us; the launch traced here: 24.7 us
  Pallas kernels  23.9 us (96%)
  local copies, waits for them, and re-layouts  0.71 us (3%)
    pallas_call x1, Pallas kernels, body(): pl.pallas_call(functools.partial(kernel, count), out_shape=jax.ShapeDtype...  23.9 us
    unnamed x1, local copies, waits for them, and re-layouts  0.71 us

profile of v3, /device:TPU:1, one launch (start us, length us, event | category | flops | bytes accessed | tf_op | source)
XLA Modules:
  0.0 24.7 jit_solution(12596946412881951078)
XLA Ops:
  0.0 23.9 %shard_map.28 = f32[256,256]{1,0:T(8,128)S(1)} custom-call(f32[2,1024,256]{2,1,0:T(8,128)} %x_ref.1, bf16[4560,640]{1,0:T(8,128)(2,1)} %constant.2.clone.const_ref), custom_call_target="tpu_custom_call" | custom-call | tf_op jit(solution)/shard_map/pallas_call | solution.py:515
  24.0 0.7 %copy.4 = f32[256,256]{1,0:T(8,128)} copy(f32[256,256]{1,0:T(8,128)S(1)} %shard_map.28) | data formatting | bytes 524288

commit v4 on v3

--- a/solution.py
+++ b/solution.py
@@ -27,12 +27,15 @@
 EXT = 67
 WIDE = 640
 ROW_PART = MID + LOW + BLOCK
-COL_PART = 3 * 256
+COL_PART = 2 * 256
 REST = 4 * ROW_PART + 3 * COL_PART
 LATE = KEEP2 + SUB // 2
 EDGE = 76
 VMEM_BYTES = 52 * 1024 * 1024
-GATE = 3
+TO_RIGHT = 72
+TO_LEFT = 80
+PART = 48
+GATE = 1
 EXPO = float(-4.0 * np.log2(np.e))
 
 
@@ -90,7 +93,7 @@
     n = 3 * COLS
     c0, c1 = reduce_matrix(n), reduce_matrix(n // 2)
     x0 = expand_matrix(n // 2)
-    col_in, col_halo, col_up = [], [], []
+    col_in, col_up = [], []
     for b in range(3):
         full = np.concatenate(
             [
@@ -99,21 +102,33 @@
                 window(c1 @ c0, 64 * b - 1, 67, 0, n),
                 window(c0, 128 * b - 1, 1, 0, n),
                 window(c0, 128 * (b + 1), 1, 0, n),
-                np.zeros((59, n)),
+                np.zeros((3, n)),
+                window(c0, 128 * (b + 1) - 1, 2, 0, n),
+                window(c1 @ c0, 64 * (b + 1) - 1, 2, 0, n),
+                np.zeros((4, n)),
+                window(c0, 128 * b - 1, 2, 0, n),
+                window(c1 @ c0, 64 * b - 1, 3, 0, n),
+                np.zeros((43, n)),
             ],
             0,
         ).T
         col_in.append(full[COLS * b : COLS * (b + 1)])
-        halo = np.zeros((128, 512))
-        halo[:16] = window(full, COLS * b - 16, 16, 0, 512)
-        halo[16:32] = window(full, COLS * (b + 1), 16, 0, 512)
-        col_halo.append(np.concatenate([halo, halo], 0))
         up = x0[COLS * b : COLS * (b + 1)].T
         both = np.zeros((256, COLS))
         both[:128] = up[128 * b : 128 * (b + 1)]
         both[128 + EXT] = window(up, 128 * b - 1, 1, 0, COLS)[0]
         both[128 + EXT + 1] = window(up, 128 * (b + 1), 1, 0, COLS)[0]
         col_up.append(both)
+    col_halo = np.zeros((128, 512))
+    for lane, i in ((0, -1), (1, 0), (8, 127), (9, 128)):
+        col_halo[lane, :COLS] = x0[COLS : 2 * COLS, 128 + i]
+        if 0 <= i < 128:
+            col_halo[lane, COLS + i] = 1.0
+        else:
+            col_halo[lane, COLS + 128 + EXT + (i > 0)] = 1.0
+    col_halo[1, COLS + 128 + 2] = TAPS[0]
+    for lane, i in ((2, -1), (3, 0), (10, 63), (11, 64), (12, 65)):
+        col_halo[lane, COLS + 128 + 1 + i] = 1.0
     col_base = np.zeros((128, 256))
     base = expand_matrix(n // 4)
     col_base[:67, :128] = window(base, 128, 128, 63, 67).T
@@ -123,8 +138,8 @@
     for p in range(4):
         parts += [row_in[p], row_low[p], row_up[p]]
     for b in range(3):
-        parts += [col_in[b], col_halo[b], col_up[b]]
-    parts += [col_base, row_base, row_sub]
+        parts += [col_in[b], col_up[b]]
+    parts += [col_base, row_base, row_sub, col_halo]
     return np.concatenate([exact(np.pad(m, ((0, 0), (0, WIDE - m.shape[1])))) for m in parts], 0)
 
 
@@ -155,10 +170,10 @@
     count,
     x_ref, const_ref,
     out_ref,
-    xwin, m_row_in, m_row_low, m_row_up, m_row_sub, m_row_base, m_col_in, m_col_halo, m_col_up, m_col_base,
-    hr, pack, halo, wide, c1, low,
+    xwin, xpart, m_row_part, m_row_in, m_row_low, m_row_up, m_row_sub, m_row_base, m_col_in, m_col_halo, m_col_up, m_col_base,
+    keep, pack, halo, wide, c1, low, part, part_in,
     level0, level1, late, far0, far1, far_late, jbuf, upper,
-    m_sem, x_sem, swap_send, swap_recv, halo_send, halo_recv, far_send, far_recv, group_sem, beside_sem,
+    m_sem, x_sem, part_send, part_recv, swap_send, swap_recv, halo_send, halo_recv, far_send, far_recv, group_sem, beside_sem,
 ):
     me = lax.axis_index("plane")
     q = lax.axis_index("col")
@@ -170,6 +185,7 @@
     left, right = (q + count - 1) % count, (q + 1) % count
     has_left, has_right = q > 0, q < count - 1
     blocks = (far, me)
+    first = 2 * (1 - chip) + 1
 
     def start_of(p):
         return pl.multiple_of(BLOCK * p - 16 + 16 * ((3 - p) // 3) - 16 * (p // 3), 16)
@@ -197,55 +213,78 @@
         (const(ROW_PART * far + MID, LOW, 384), m_row_low.at[0]),
         (const(REST, 128, 256), m_col_base),
         (const(REST + 128, MID, 256), m_row_base),
-        (const(col_at + 256, 256, 512), m_col_halo),
+        (const(REST + 128 + MID + SUB, 128, 512), m_col_halo),
         (const(ROW_PART * me + MID, LOW, 384), m_row_low.at[1]),
-        (const(col_at + 512, 256, 256), m_col_up),
+        (const(col_at + 256, 256, 256), m_col_up),
         (const(ROW_PART * me + MID + LOW, BLOCK, 384), m_row_up),
+        (const(ROW_PART * first, PART, 128), m_row_part),
     ]
     loads = [pltpu.make_async_copy(s, d, m_sem.at[i]) for i, (s, d) in enumerate(loads)]
+    early = pltpu.make_async_copy(x_ref.at[:, pl.ds(start_of(first), 128)], xpart, x_sem.at[2])
+    early.start()
+    loads[11].start()
+    loads[2].start()
+    loads[3].start()
     own[0].start()
     loads[0].start()
-    loads[2].start()
-    loads[3].start()
 
     barrier = pltpu.get_barrier_semaphore()
 
     def tell(sem, plane, col):
         pl.semaphore_signal(sem, inc=1, device_id=(plane, col), device_id_type=MESH)
 
-    @pl.when(sibling != GATE)
-    def _():
-        tell(barrier, sibling, q)
-
-    @pl.when(far != GATE)
-    def _():
-        tell(barrier, far, q)
+    def enter(plane):
+        @pl.when(plane != GATE)
+        def _():
+            tell(barrier, plane, q)
+
+    for plane in (sibling, far, far_sibling):
+        enter(plane)
 
     own[1].start()
     loads[1].start()
-    for copy in loads[4:]:
+    for copy in loads[4:11]:
         copy.start()
     jbuf[pl.ds(KEEP, MID - KEEP)] = jnp.zeros((MID - KEEP, COLS), F32)
 
     @pl.when(q == 0)
     def _():
-        halo[0] = jnp.zeros((MID, 128), F32)
+        halo[0] = jnp.zeros((MID // 2, 128), F32)
 
     @pl.when(q == count - 1)
     def _():
-        halo[1] = jnp.zeros((MID, 128), F32)
+        halo[1] = jnp.zeros((MID // 2, 128), F32)
+
+    def twice(ref):
+        m = ref[...]
+        return jnp.concatenate([m, m], 0)
+
+    early.wait()
+    for i in (11, 2, 3):
+        loads[i].wait()
+    num = jnp.zeros((SUB, COLS), F32)
+    den = jnp.zeros((SUB, COLS), F32)
+    for p in range(2):
+        m = m_row_part[...]
+        value = dot(jnp.concatenate([m, m], 1), tall(xpart[p]))
+        m = m_col_in[:, pl.ds(0, COLS)]
+        value = dot(jnp.concatenate(split(value), 1), jnp.concatenate([m, m], 0))
+        z = dot(m_row_sub[:, pl.ds(0, 2 * PART)], tall(value))
+        d = xpart[p, pl.ds(offset_of(first), SUB)] - z
+        w = weight(d)
+        num = num + w * d
+        den = den + w
+    part[0] = num
+    part[1] = den
 
     @pl.when(me != GATE)
     def _():
-        pl.semaphore_wait(barrier, 2)
-
-    @pl.when((sibling == GATE) | (far == GATE))
-    def _():
+        pl.semaphore_wait(barrier, 3)
         tell(group_sem, GATE, q)
 
     @pl.when(me == GATE)
     def _():
-        pl.semaphore_wait(group_sem, 2)
+        pl.semaphore_wait(group_sem, 3)
 
         @pl.when(has_left)
         def _():
@@ -272,10 +311,13 @@
                 q,
             )
         )
-    for copy in swaps:
-        copy.start()
+    far_part = remote(part, part_in.at[core], part_send.at[0], part_recv.at[core], first, q)
+    swaps[0].start()
+    far_part.start()
+    swaps[1].start()
 
     lane = lax.broadcasted_iota(jnp.int32, (MID, 128), 1)
+    fold_lane = lax.broadcasted_iota(jnp.int32, (MID // 2, 128), 1)
     half_lane = lax.broadcasted_iota(jnp.int32, (SUB // 2, 128), 1)
     sub_lane = lax.broadcasted_iota(jnp.int32, (SUB, 128), 1)
     low_lane = lax.broadcasted_iota(jnp.int32, (KEEP2, 128), 1)
@@ -292,7 +334,8 @@
         if p == 2:
             swaps[b].wait_recv()
         value = dot(m_row_in[b, :, pl.ds(0, 2 * WIN)], tall(xwin[b, p]))
-        hr[b, p] = value
+        value = dot(jnp.concatenate(split(value), 1), twice(m_col_in))
+        keep[b, p] = value
         return value
 
     def put(p, value):
@@ -314,10 +357,6 @@
             num = num + w * d
             den = den + w
         return num, den
-
-    def twice(ref):
-        m = ref[...]
-        return jnp.concatenate([m, m], 0)
 
     def columns_up(c2):
         return dot(jnp.concatenate(split(c2), 1), twice(m_col_base))
@@ -357,29 +396,28 @@
     far_one = remote(level1.at[0], far1, far_send.at[SUBS], far_recv.at[SUBS], far, q)
     far_last = remote(late.at[0], far_late, far_send.at[SUBS + 1], far_recv.at[SUBS + 1], far, q)
     for p in range(4):
-        value = rows_in(0, p)
-        if p == 0:
-            loads[2].wait()
-            loads[3].wait()
-        put(p, dot(jnp.concatenate(split(value), 1), twice(m_col_in)))
+        put(p, rows_in(0, p))
 
     def far_chunk(s):
         num, den = sums_zero(0, s)
         level0[0, s, 0] = num
         level0[0, s, 1] = den
-        if s < SUBS - 1:
-            far_zero[s].start()
-
-    far_chunk(0)
+
+    for s in range(1, SUBS - 1):
+        far_chunk(s)
+        pl.when(core == 1)(far_zero[s].start)
     for p in range(4):
         rows_in(1, p)
-    packs = [jnp.zeros((MID, 128), F32), jnp.zeros((MID, 128), F32)]
+    packs = [jnp.zeros((MID // 2, 128), F32), jnp.zeros((MID // 2, 128), F32)]
     for b in range(2):
         for p in range(4):
-            at = 64 * b + 16 * p
-            here = (lane >= at) & (lane < at + 16)
-            packs[0] = jnp.where(here, turn(hr[b, p, :, pl.ds(0, 128)], at), packs[0])
-            packs[1] = jnp.where(here, turn(hr[b, p, :, pl.ds(128, 128)], 16 + at), packs[1])
+            tile = keep[b, p, :, pl.ds(COLS + 128, 128)]
+            for h in range(2):
+                at = 64 * h + 32 * b + 8 * p
+                here = (fold_lane >= at) & (fold_lane < at + 8)
+                rows = tile[MID // 2 * h : MID // 2 * (h + 1)]
+                packs[0] = jnp.where(here, turn(rows, at - TO_LEFT), packs[0])
+                packs[1] = jnp.where(here, turn(rows, at - TO_RIGHT), packs[1])
     pack[0] = packs[0]
     pack[1] = packs[1]
 
@@ -390,7 +428,7 @@
         @pl.when(me == GATE)
         def _():
             pl.semaphore_wait(barrier, (q + count - 1) // count + (2 * count - 2 - q) // count)
-            for plane in range(GATE):
+            for plane in (0, 2, 3):
                 tell(beside_sem, plane, q)
 
         @pl.when(me != GATE)
@@ -408,8 +446,10 @@
     ahead = q % 8 == 0
     pl.when(jnp.logical_not(ahead))(send_halo)
 
-    for s in range(1, SUBS):
-        far_chunk(s)
+    far_chunk(0)
+    for s in range(SUBS - 1):
+        pl.when(core == 0)(far_zero[s].start)
+    far_chunk(SUBS - 1)
     for copy in loads[4:7]:
         copy.wait()
     num, den, _ = sums_one(0)
@@ -417,8 +457,9 @@
     far_one.start()
 
     pl.when(ahead)(send_halo)
-
-    for copy in loads[7:]:
+    pl.when(ahead)(far_zero[SUBS - 1].start)
+
+    for copy in loads[7:11]:
         copy.wait()
 
     @pl.when(has_left)
@@ -431,10 +472,11 @@
 
     for b in range(2):
         for p in range(4):
-            at = 64 * b + 16 * p
-            edge = jnp.where(lane < 16, turn(halo[0], -at), jnp.where(lane < 32, turn(halo[1], 16 - at), 0.0))
-            lhs = jnp.concatenate(split(hr[b, p]) + split(edge), 1)
-            put(p, dot(lhs, jnp.concatenate([twice(m_col_in), m_col_halo[...]], 0)))
+            at = 32 * b + 8 * p
+            from_left = jnp.concatenate([turn(halo[0], -at), turn(halo[0], -at - 64)], 0)
+            from_right = jnp.concatenate([turn(halo[1], 8 - at), turn(halo[1], 8 - at - 64)], 0)
+            edge = jnp.where(lane < 8, from_left, jnp.where(lane < 16, from_right, 0.0))
+            put(p, keep[b, p] + dot(jnp.concatenate(split(edge), 1), twice(m_col_halo)))
 
         num, den, total = sums_one(b)
         late[b, pl.ds(0, KEEP2)] = late_tile(num, den, total)
@@ -457,7 +499,7 @@
         if b == 0:
             late[0, pl.ds(KEEP2, SUB // 2)] = patch
             far_last.start()
-            far_zero[SUBS - 1].start()
+            pl.when(jnp.logical_not(ahead))(far_zero[SUBS - 1].start)
 
     far_one.wait_recv()
     far_last.wait_recv()
@@ -480,9 +522,17 @@
     u = dot(jnp.concatenate(split(jbuf[...]), 1), twice(m_col_up))
     upper[...] = dot(m_row_up[:, pl.ds(0, 2 * MID)], tall(u))
 
+    @pl.when(core == 1)
+    def _():
+        for i in range(2):
+            remote(part, part_in.at[i], part_send.at[0], part_recv.at[i], first, q).wait_recv()
+        far0[0] = part_in[0] + part_in[1]
+
+    pl.when(core == 0)(far_zero[0].wait_recv)
     patch = far_late[pl.ds(KEEP2, SUB // 2)]
     for s in range(SUBS):
-        far_zero[s].wait_recv()
+        if s:
+            far_zero[s].wait_recv()
         sums = []
         for i in range(2):
             at = 32 * s + 8 * i
@@ -501,7 +551,8 @@
     def _():
         to_right.wait_send()
 
-    for copy in swaps + far_zero + [far_one, far_last]:
+    pl.when(core == 0)(far_zero[0].wait_send)
+    for copy in swaps + far_zero[1:] + [far_one, far_last, far_part]:
         copy.wait_send()
 
 
@@ -519,21 +570,25 @@
             out_specs=pl.BlockSpec(memory_space=pltpu.VMEM),
             scratch_shapes=[
                 vmem((2, 4, WIN, COLS), F32),
+                vmem((2, 128, COLS), F32),
+                vmem((PART, 128), BF),
                 vmem((2, MID, WIDE), BF),
                 vmem((2, LOW, 384), BF),
                 vmem((BLOCK, 384), BF),
                 vmem((SUB, 128), BF),
                 vmem((MID, 256), BF),
                 vmem((256, 512), BF),
-                vmem((256, 512), BF),
+                vmem((128, 512), BF),
                 vmem((256, 256), BF),
                 vmem((128, 256), BF),
-                vmem((2, 4, MID, COLS), F32),
-                vmem((2, MID, 128), F32),
-                vmem((2, MID, 128), F32),
+                vmem((2, 4, MID, 512), F32),
+                vmem((2, MID // 2, 128), F32),
+                vmem((2, MID // 2, 128), F32),
                 vmem((4, 2, MID, COLS), BF),
                 vmem((4, MID, 128), F32),
                 vmem((MID, 512), F32),
+                vmem((2, SUB, COLS), F32),
+                vmem((2, 2, SUB, COLS), F32),
                 vmem((2, SUBS, 2, SUB, COLS), F32),
                 vmem((2, 2, KEEP, 128), F32),
                 vmem((2, LATE, 128), F32),
@@ -542,7 +597,9 @@
                 vmem((LATE, 128), F32),
                 vmem((MID, COLS), F32),
                 vmem((BLOCK, COLS), F32),
-                dma((11,)),
+                dma((12,)),
+                dma((3,)),
+                dma((1,)),
                 dma((2,)),
                 dma((2,)),
                 dma((2,)),

time: 24.8 us -> 25.1 us (1.012)
  the two profiles are of different devices: /device:TPU:1 before, /device:TPU:4 now
where the time goes in v4:
time: 25.1 us; the launch traced here: 25 us
  Pallas kernels  24.3 us (97%)
  local copies, waits for them, and re-layouts  0.71 us (3%)
    pallas_call x1, Pallas kernels, body(): pl.pallas_call(functools.partial(kernel, count), out_shape=jax.ShapeDtype...  24.3 us
    unnamed x1, local copies, waits for them, and re-layouts  0.71 us

profile of v4, /device:TPU:4, one launch (start us, length us, event | category | flops | bytes accessed | tf_op | source)
XLA Modules:
  0.0 25.0 jit_solution(8099710643732120492)
XLA Ops:
  0.0 24.3 %shard_map.28 = f32[256,256]{1,0:T(8,128)S(1)} custom-call(f32[2,1024,256]{2,1,0:T(8,128)} %x_ref.1, bf16[3920,640]{1,0:T(8,128)(2,1)} %constant.2.clone.const_ref), custom_call_target="tpu_custom_call" | custom-call | tf_op jit(solution)/shard_map/pallas_call | solution.py:566
  24.3 0.7 %copy.4 = f32[256,256]{1,0:T(8,128)} copy(f32[256,256]{1,0:T(8,128)S(1)} %shard_map.28) | data formatting | bytes 524288

commit v5 on v4

--- a/solution.py
+++ b/solution.py
@@ -259,6 +259,43 @@
         m = ref[...]
         return jnp.concatenate([m, m], 0)
 
+    @pl.when(me != GATE)
+    def _():
+        pl.semaphore_wait(barrier, 3)
+        tell(group_sem, GATE, q)
+
+    @pl.when(me == GATE)
+    def _():
+        pl.semaphore_wait(group_sem, 3)
+
+        @pl.when(has_left)
+        def _():
+            tell(barrier, GATE, left)
+
+        @pl.when(has_right)
+        def _():
+            tell(barrier, GATE, right)
+
+    def remote(src, dst, send, recv, plane, col):
+        return pltpu.make_async_remote_copy(
+            src_ref=src, dst_ref=dst, send_sem=send, recv_sem=recv, device_id=(plane, col), device_id_type=MESH
+        )
+
+    swaps = []
+    for b, p in enumerate((far_sibling, sibling)):
+        swaps.append(
+            remote(
+                x_ref.at[:, pl.ds(start_of(p), WIN)],
+                xwin.at[b, pl.ds(2, 2)],
+                swap_send.at[b],
+                swap_recv.at[b],
+                sibling,
+                q,
+            )
+        )
+    for copy in swaps:
+        copy.start()
+
     early.wait()
     for i in (11, 2, 3):
         loads[i].wait()
@@ -277,44 +314,8 @@
     part[0] = num
     part[1] = den
 
-    @pl.when(me != GATE)
-    def _():
-        pl.semaphore_wait(barrier, 3)
-        tell(group_sem, GATE, q)
-
-    @pl.when(me == GATE)
-    def _():
-        pl.semaphore_wait(group_sem, 3)
-
-        @pl.when(has_left)
-        def _():
-            tell(barrier, GATE, left)
-
-        @pl.when(has_right)
-        def _():
-            tell(barrier, GATE, right)
-
-    def remote(src, dst, send, recv, plane, col):
-        return pltpu.make_async_remote_copy(
-            src_ref=src, dst_ref=dst, send_sem=send, recv_sem=recv, device_id=(plane, col), device_id_type=MESH
-        )
-
-    swaps = []
-    for b, p in enumerate((far_sibling, sibling)):
-        swaps.append(
-            remote(
-                x_ref.at[:, pl.ds(start_of(p), WIN)],
-                xwin.at[b, pl.ds(2, 2)],
-                swap_send.at[b],
-                swap_recv.at[b],
-                sibling,
-                q,
-            )
-        )
     far_part = remote(part, part_in.at[core], part_send.at[0], part_recv.at[core], first, q)
-    swaps[0].start()
     far_part.start()
-    swaps[1].start()
 
     lane = lax.broadcasted_iota(jnp.int32, (MID, 128), 1)
     fold_lane = lax.broadcasted_iota(jnp.int32, (MID // 2, 128), 1)
@@ -326,6 +327,15 @@
     def turn(v, by):
         by = by % 128
         return pltpu.roll(v, by, 1) if by else v
+
+    ahead = q % 8 == 0
+
+    def meet():
+        @pl.when(me == GATE)
+        def _():
+            pl.semaphore_wait(barrier, (q + count - 1) // count + (2 * count - 2 - q) // count)
+            for plane in (0, 2, 3):
+                tell(beside_sem, plane, q)
 
     def rows_in(b, p):
         if p == 0:
@@ -396,6 +406,8 @@
     far_one = remote(level1.at[0], far1, far_send.at[SUBS], far_recv.at[SUBS], far, q)
     far_last = remote(late.at[0], far_late, far_send.at[SUBS + 1], far_recv.at[SUBS + 1], far, q)
     for p in range(4):
+        if p == 2:
+            pl.when(jnp.logical_not(ahead))(meet)
         put(p, rows_in(0, p))
 
     def far_chunk(s):
@@ -425,12 +437,6 @@
     to_right = remote(pack.at[1], halo.at[0], halo_send.at[1], halo_recv.at[0], me, right)
 
     def send_halo():
-        @pl.when(me == GATE)
-        def _():
-            pl.semaphore_wait(barrier, (q + count - 1) // count + (2 * count - 2 - q) // count)
-            for plane in (0, 2, 3):
-                tell(beside_sem, plane, q)
-
         @pl.when(me != GATE)
         def _():
             pl.semaphore_wait(beside_sem, 1)
@@ -443,7 +449,6 @@
         def _():
             to_right.start()
 
-    ahead = q % 8 == 0
     pl.when(jnp.logical_not(ahead))(send_halo)
 
     far_chunk(0)
@@ -456,6 +461,7 @@
     put_one(0, num, den)
     far_one.start()
 
+    pl.when(ahead)(meet)
     pl.when(ahead)(send_halo)
     pl.when(ahead)(far_zero[SUBS - 1].start)
 

time: 25.1 us -> 24.7 us (0.984)
  the two profiles are of different devices: /device:TPU:4 before, /device:TPU:2 now
where the time goes in v5:
time: 24.7 us; the launch traced here: 24.6 us
  Pallas kernels  23.9 us (97%)
  local copies, waits for them, and re-layouts  0.71 us (3%)
    pallas_call x1, Pallas kernels, body(): pl.pallas_call(functools.partial(kernel, count), out_shape=jax.ShapeDtype...  23.9 us
    unnamed x1, local copies, waits for them, and re-layouts  0.71 us

profile of v5, /device:TPU:2, one launch (start us, length us, event | category | flops | bytes accessed | tf_op | source)
XLA Modules:
  0.0 24.6 jit_solution(14041219174324680280)
XLA Ops:
  0.0 23.9 %shard_map.28 = f32[256,256]{1,0:T(8,128)S(1)} custom-call(f32[2,1024,256]{2,1,0:T(8,128)} %x_ref.1, bf16[3920,640]{1,0:T(8,128)(2,1)} %constant.2.clone.const_ref), custom_call_target="tpu_custom_call" | custom-call | tf_op jit(solution)/shard_map/pallas_call | solution.py:572
  23.9 0.7 %copy.4 = f32[256,256]{1,0:T(8,128)} copy(f32[256,256]{1,0:T(8,128)S(1)} %shard_map.28) | data formatting | bytes 524288

commit v6 on v5

--- a/solution.py
+++ b/solution.py
@@ -35,6 +35,7 @@
 TO_RIGHT = 72
 TO_LEFT = 80
 PART = 48
+OWN = 48
 GATE = 1
 EXPO = float(-4.0 * np.log2(np.e))
 
@@ -293,21 +294,20 @@
                 q,
             )
         )
-    for copy in swaps:
-        copy.start()
+    swaps[0].start()
 
     early.wait()
     for i in (11, 2, 3):
         loads[i].wait()
-    num = jnp.zeros((SUB, COLS), F32)
-    den = jnp.zeros((SUB, COLS), F32)
+    num = jnp.zeros((OWN, COLS), F32)
+    den = jnp.zeros((OWN, COLS), F32)
     for p in range(2):
         m = m_row_part[...]
         value = dot(jnp.concatenate([m, m], 1), tall(xpart[p]))
         m = m_col_in[:, pl.ds(0, COLS)]
         value = dot(jnp.concatenate(split(value), 1), jnp.concatenate([m, m], 0))
-        z = dot(m_row_sub[:, pl.ds(0, 2 * PART)], tall(value))
-        d = xpart[p, pl.ds(offset_of(first), SUB)] - z
+        z = dot(m_row_sub[pl.ds(0, OWN), pl.ds(0, 2 * PART)], tall(value))
+        d = xpart[p, pl.ds(offset_of(first), OWN)] - z
         w = weight(d)
         num = num + w * d
         den = den + w
@@ -316,6 +316,7 @@
 
     far_part = remote(part, part_in.at[core], part_send.at[0], part_recv.at[core], first, q)
     far_part.start()
+    swaps[1].start()
 
     lane = lax.broadcasted_iota(jnp.int32, (MID, 128), 1)
     fold_lane = lax.broadcasted_iota(jnp.int32, (MID // 2, 128), 1)
@@ -328,7 +329,7 @@
         by = by % 128
         return pltpu.roll(v, by, 1) if by else v
 
-    ahead = q % 8 == 0
+    ahead = (q % 8 == 0) & has_left
 
     def meet():
         @pl.when(me == GATE)
@@ -403,6 +404,8 @@
         return tile
 
     far_zero = [remote(level0.at[0, s], far0.at[s], far_send.at[s], far_recv.at[s], far, q) for s in range(SUBS)]
+    rest = pl.ds(OWN, SUB - OWN)
+    far_rest = remote(level0.at[0, 0, :, rest], far0.at[0, :, rest], far_send.at[0], far_recv.at[0], far, q)
     far_one = remote(level1.at[0], far1, far_send.at[SUBS], far_recv.at[SUBS], far, q)
     far_last = remote(late.at[0], far_late, far_send.at[SUBS + 1], far_recv.at[SUBS + 1], far, q)
     for p in range(4):
@@ -418,6 +421,8 @@
     for s in range(1, SUBS - 1):
         far_chunk(s)
         pl.when(core == 1)(far_zero[s].start)
+    far_chunk(0)
+    pl.when(core == 1)(far_rest.start)
     for p in range(4):
         rows_in(1, p)
     packs = [jnp.zeros((MID // 2, 128), F32), jnp.zeros((MID // 2, 128), F32)]
@@ -451,7 +456,6 @@
 
     pl.when(jnp.logical_not(ahead))(send_halo)
 
-    far_chunk(0)
     for s in range(SUBS - 1):
         pl.when(core == 0)(far_zero[s].start)
     far_chunk(SUBS - 1)
@@ -463,7 +467,6 @@
 
     pl.when(ahead)(meet)
     pl.when(ahead)(send_halo)
-    pl.when(ahead)(far_zero[SUBS - 1].start)
 
     for copy in loads[7:11]:
         copy.wait()
@@ -505,7 +508,7 @@
         if b == 0:
             late[0, pl.ds(KEEP2, SUB // 2)] = patch
             far_last.start()
-            pl.when(jnp.logical_not(ahead))(far_zero[SUBS - 1].start)
+            far_zero[SUBS - 1].start()
 
     far_one.wait_recv()
     far_last.wait_recv()
@@ -532,7 +535,8 @@
     def _():
         for i in range(2):
             remote(part, part_in.at[i], part_send.at[0], part_recv.at[i], first, q).wait_recv()
-        far0[0] = part_in[0] + part_in[1]
+        far_rest.wait_recv()
+        far0[0, :, pl.ds(0, OWN)] = part_in[0] + part_in[1]
 
     pl.when(core == 0)(far_zero[0].wait_recv)
     patch = far_late[pl.ds(KEEP2, SUB // 2)]
@@ -558,6 +562,7 @@
         to_right.wait_send()
 
     pl.when(core == 0)(far_zero[0].wait_send)
+    pl.when(core == 1)(far_rest.wait_send)
     for copy in swaps + far_zero[1:] + [far_one, far_last, far_part]:
         copy.wait_send()
 
@@ -593,8 +598,8 @@
                 vmem((4, 2, MID, COLS), BF),
                 vmem((4, MID, 128), F32),
                 vmem((MID, 512), F32),
-                vmem((2, SUB, COLS), F32),
-                vmem((2, 2, SUB, COLS), F32),
+                vmem((2, OWN, COLS), F32),
+                vmem((2, 2, OWN, COLS), F32),
                 vmem((2, SUBS, 2, SUB, COLS), F32),
                 vmem((2, 2, KEEP, 128), F32),
                 vmem((2, LATE, 128), F32),

time: 24.7 us -> 24.6 us (level)
  the two profiles are of different devices: /device:TPU:2 before, /device:TPU:4 now
where the time goes in v6:
time: 24.6 us; the launch traced here: 24.5 us
  Pallas kernels  23.8 us (97%)
  local copies, waits for them, and re-layouts  0.71 us (3%)
    pallas_call x1, Pallas kernels, body(): pl.pallas_call(functools.partial(kernel, count), out_shape=jax.ShapeDtype...  23.8 us
    unnamed x1, local copies, waits for them, and re-layouts  0.71 us

profile of v6, /device:TPU:4, one launch (start us, length us, event | category | flops | bytes accessed | tf_op | source)
XLA Modules:
  0.0 24.5 jit_solution(694950554591138717)
XLA Ops:
  0.0 23.8 %shard_map.28 = f32[256,256]{1,0:T(8,128)S(1)} custom-call(f32[2,1024,256]{2,1,0:T(8,128)} %x_ref.1, bf16[3920,640]{1,0:T(8,128)(2,1)} %constant.2.clone.const_ref), custom_call_target="tpu_custom_call" | custom-call | tf_op jit(solution)/shard_map/pallas_call | solution.py:577
  23.8 0.7 %copy.4 = f32[256,256]{1,0:T(8,128)} copy(f32[256,256]{1,0:T(8,128)S(1)} %shard_map.28) | data formatting | bytes 524288

commit v7 on v6

--- a/solution.py
+++ b/solution.py
@@ -174,7 +174,7 @@
     xwin, xpart, m_row_part, m_row_in, m_row_low, m_row_up, m_row_sub, m_row_base, m_col_in, m_col_halo, m_col_up, m_col_base,
     keep, pack, halo, wide, c1, low, part, part_in,
     level0, level1, late, far0, far1, far_late, jbuf, upper,
-    m_sem, x_sem, part_send, part_recv, swap_send, swap_recv, halo_send, halo_recv, far_send, far_recv, group_sem, beside_sem,
+    m_sem, x_sem, part_send, part_recv, swap_send, swap_recv, halo_send, halo_recv, far_send, far_recv, group_sem, sibling_sem, far_sem, beside_sem,
 ):
     me = lax.axis_index("plane")
     q = lax.axis_index("col")
@@ -187,6 +187,20 @@
     has_left, has_right = q > 0, q < count - 1
     blocks = (far, me)
     first = 2 * (1 - chip) + 1
+
+    barrier = pltpu.get_barrier_semaphore()
+
+    def tell(sem, plane, col):
+        pl.semaphore_signal(sem, inc=1, device_id=(plane, col), device_id_type=MESH)
+
+    @pl.when(me == GATE)
+    def _():
+        for plane in (0, 2, 3):
+            tell(barrier, plane, q)
+
+    @pl.when((me == 0) | (me == 3))
+    def _():
+        tell(barrier, 2, q)
 
     def start_of(p):
         return pl.multiple_of(BLOCK * p - 16 + 16 * ((3 - p) // 3) - 16 * (p // 3), 16)
@@ -229,53 +243,28 @@
     own[0].start()
     loads[0].start()
 
-    barrier = pltpu.get_barrier_semaphore()
-
-    def tell(sem, plane, col):
-        pl.semaphore_signal(sem, inc=1, device_id=(plane, col), device_id_type=MESH)
-
-    def enter(plane):
-        @pl.when(plane != GATE)
-        def _():
-            tell(barrier, plane, q)
-
-    for plane in (sibling, far, far_sibling):
-        enter(plane)
-
-    own[1].start()
-    loads[1].start()
-    for copy in loads[4:11]:
-        copy.start()
-    jbuf[pl.ds(KEEP, MID - KEEP)] = jnp.zeros((MID - KEEP, COLS), F32)
-
-    @pl.when(q == 0)
-    def _():
-        halo[0] = jnp.zeros((MID // 2, 128), F32)
-
-    @pl.when(q == count - 1)
-    def _():
-        halo[1] = jnp.zeros((MID // 2, 128), F32)
-
     def twice(ref):
         m = ref[...]
         return jnp.concatenate([m, m], 0)
 
-    @pl.when(me != GATE)
+    @pl.when((me == 0) | (me == 3))
+    def _():
+        pl.semaphore_wait(barrier, 1)
+
+    @pl.when(me == 2)
     def _():
         pl.semaphore_wait(barrier, 3)
+        tell(sibling_sem, 3, q)
+        tell(far_sem, 0, q)
         tell(group_sem, GATE, q)
 
-    @pl.when(me == GATE)
-    def _():
-        pl.semaphore_wait(group_sem, 3)
-
-        @pl.when(has_left)
-        def _():
-            tell(barrier, GATE, left)
-
-        @pl.when(has_right)
-        def _():
-            tell(barrier, GATE, right)
+    @pl.when(me == 0)
+    def _():
+        tell(sibling_sem, GATE, q)
+
+    @pl.when(me == 3)
+    def _():
+        tell(far_sem, GATE, q)
 
     def remote(src, dst, send, recv, plane, col):
         return pltpu.make_async_remote_copy(
@@ -294,7 +283,25 @@
                 q,
             )
         )
+    @pl.when(core == 1)
+    def _():
+        pl.semaphore_wait(sibling_sem, 1)
+
     swaps[0].start()
+
+    own[1].start()
+    loads[1].start()
+    for copy in loads[4:11]:
+        copy.start()
+    jbuf[pl.ds(KEEP, MID - KEEP)] = jnp.zeros((MID - KEEP, COLS), F32)
+
+    @pl.when(q == 0)
+    def _():
+        halo[0] = jnp.zeros((MID // 3, 128), F32)
+
+    @pl.when(q == count - 1)
+    def _():
+        halo[1] = jnp.zeros((MID // 3, 128), F32)
 
     early.wait()
     for i in (11, 2, 3):
@@ -305,7 +312,8 @@
         m = m_row_part[...]
         value = dot(jnp.concatenate([m, m], 1), tall(xpart[p]))
         m = m_col_in[:, pl.ds(0, COLS)]
-        value = dot(jnp.concatenate(split(value), 1), jnp.concatenate([m, m], 0))
+        value = dot(jnp.concatenate(split(value), 0), m)
+        value = value[:PART] + value[PART:]
         z = dot(m_row_sub[pl.ds(0, OWN), pl.ds(0, 2 * PART)], tall(value))
         d = xpart[p, pl.ds(offset_of(first), OWN)] - z
         w = weight(d)
@@ -315,11 +323,28 @@
     part[1] = den
 
     far_part = remote(part, part_in.at[core], part_send.at[0], part_recv.at[core], first, q)
+
+    @pl.when(chip == 0)
+    def _():
+        pl.semaphore_wait(far_sem, 1)
+
     far_part.start()
     swaps[1].start()
 
+    @pl.when(me == GATE)
+    def _():
+        pl.semaphore_wait(group_sem, 1)
+
+        @pl.when(has_left)
+        def _():
+            tell(barrier, GATE, left)
+
+        @pl.when(has_right)
+        def _():
+            tell(barrier, GATE, right)
+
     lane = lax.broadcasted_iota(jnp.int32, (MID, 128), 1)
-    fold_lane = lax.broadcasted_iota(jnp.int32, (MID // 2, 128), 1)
+    fold_lane = lax.broadcasted_iota(jnp.int32, (MID // 3, 128), 1)
     half_lane = lax.broadcasted_iota(jnp.int32, (SUB // 2, 128), 1)
     sub_lane = lax.broadcasted_iota(jnp.int32, (SUB, 128), 1)
     low_lane = lax.broadcasted_iota(jnp.int32, (KEEP2, 128), 1)
@@ -330,6 +355,7 @@
         return pltpu.roll(v, by, 1) if by else v
 
     ahead = (q % 8 == 0) & has_left
+    behind = (q % (count // 2) == 0) & has_left
 
     def meet():
         @pl.when(me == GATE)
@@ -344,10 +370,15 @@
             loads[b].wait()
         if p == 2:
             swaps[b].wait_recv()
-        value = dot(m_row_in[b, :, pl.ds(0, 2 * WIN)], tall(xwin[b, p]))
-        value = dot(jnp.concatenate(split(value), 1), twice(m_col_in))
-        keep[b, p] = value
-        return value
+        return dot(m_row_in[b, :, pl.ds(0, 2 * WIN)], tall(xwin[b, p]))
+
+    def columns_in(b, planes):
+        halves = []
+        for p in planes:
+            halves += split(rows_in(b, p))
+        value = dot(jnp.concatenate(halves, 0), m_col_in[...])
+        for i, p in enumerate(planes):
+            keep[b, p] = value[2 * MID * i : 2 * MID * i + MID] + value[2 * MID * i + MID : 2 * MID * (i + 1)]
 
     def put(p, value):
         whi, wlo = split(value[:, :COLS])
@@ -408,10 +439,13 @@
     far_rest = remote(level0.at[0, 0, :, rest], far0.at[0, :, rest], far_send.at[0], far_recv.at[0], far, q)
     far_one = remote(level1.at[0], far1, far_send.at[SUBS], far_recv.at[SUBS], far, q)
     far_last = remote(late.at[0], far_late, far_send.at[SUBS + 1], far_recv.at[SUBS + 1], far, q)
-    for p in range(4):
-        if p == 2:
-            pl.when(jnp.logical_not(ahead))(meet)
-        put(p, rows_in(0, p))
+    columns_in(0, (0, 1))
+    put(0, keep[0, 0])
+    put(1, keep[0, 1])
+    columns_in(1, (0, 1))
+    columns_in(0, (2, 3))
+    put(2, keep[0, 2])
+    put(3, keep[0, 3])
 
     def far_chunk(s):
         num, den = sums_zero(0, s)
@@ -423,16 +457,16 @@
         pl.when(core == 1)(far_zero[s].start)
     far_chunk(0)
     pl.when(core == 1)(far_rest.start)
-    for p in range(4):
-        rows_in(1, p)
-    packs = [jnp.zeros((MID // 2, 128), F32), jnp.zeros((MID // 2, 128), F32)]
+    pl.when(jnp.logical_not(ahead))(meet)
+    columns_in(1, (2, 3))
+    packs = [jnp.zeros((MID // 3, 128), F32), jnp.zeros((MID // 3, 128), F32)]
     for b in range(2):
         for p in range(4):
             tile = keep[b, p, :, pl.ds(COLS + 128, 128)]
-            for h in range(2):
-                at = 64 * h + 32 * b + 8 * p
-                here = (fold_lane >= at) & (fold_lane < at + 8)
-                rows = tile[MID // 2 * h : MID // 2 * (h + 1)]
+            for h in range(3):
+                at = 40 * h + 20 * b + 5 * p
+                here = (fold_lane >= at) & (fold_lane < at + 5)
+                rows = tile[MID // 3 * h : MID // 3 * (h + 1)]
                 packs[0] = jnp.where(here, turn(rows, at - TO_LEFT), packs[0])
                 packs[1] = jnp.where(here, turn(rows, at - TO_RIGHT), packs[1])
     pack[0] = packs[0]
@@ -468,6 +502,7 @@
     pl.when(ahead)(meet)
     pl.when(ahead)(send_halo)
 
+    pl.when(behind)(far_zero[SUBS - 1].start)
     for copy in loads[7:11]:
         copy.wait()
 
@@ -480,12 +515,16 @@
         to_left.wait_recv()
 
     for b in range(2):
+        edges = []
         for p in range(4):
-            at = 32 * b + 8 * p
-            from_left = jnp.concatenate([turn(halo[0], -at), turn(halo[0], -at - 64)], 0)
-            from_right = jnp.concatenate([turn(halo[1], 8 - at), turn(halo[1], 8 - at - 64)], 0)
-            edge = jnp.where(lane < 8, from_left, jnp.where(lane < 16, from_right, 0.0))
-            put(p, keep[b, p] + dot(jnp.concatenate(split(edge), 1), twice(m_col_halo)))
+            at = 20 * b + 5 * p
+            from_left = jnp.concatenate([turn(halo[0], -at - 40 * h) for h in range(3)], 0)
+            from_right = jnp.concatenate([turn(halo[1], 8 - at - 40 * h) for h in range(3)], 0)
+            edge = jnp.where((lane >= 8) & (lane < 13), from_right, jnp.where(lane < 5, from_left, 0.0))
+            edges.append(jnp.concatenate(split(edge), 1))
+        added = dot(jnp.concatenate(edges, 0), twice(m_col_halo))
+        for p in range(4):
+            put(p, keep[b, p] + added[MID * p : MID * (p + 1)])
 
         num, den, total = sums_one(b)
         late[b, pl.ds(0, KEEP2)] = late_tile(num, den, total)
@@ -508,7 +547,7 @@
         if b == 0:
             late[0, pl.ds(KEEP2, SUB // 2)] = patch
             far_last.start()
-            far_zero[SUBS - 1].start()
+            pl.when(jnp.logical_not(behind))(far_zero[SUBS - 1].start)
 
     far_one.wait_recv()
     far_last.wait_recv()
@@ -593,8 +632,8 @@
                 vmem((256, 256), BF),
                 vmem((128, 256), BF),
                 vmem((2, 4, MID, 512), F32),
-                vmem((2, MID // 2, 128), F32),
-                vmem((2, MID // 2, 128), F32),
+                vmem((2, MID // 3, 128), F32),
+                vmem((2, MID // 3, 128), F32),
                 vmem((4, 2, MID, COLS), BF),
                 vmem((4, MID, 128), F32),
                 vmem((MID, 512), F32),
@@ -620,6 +659,8 @@
                 dma((SUBS + 2,)),
                 pltpu.SemaphoreType.REGULAR,
                 pltpu.SemaphoreType.REGULAR,
+                pltpu.SemaphoreType.REGULAR,
+                pltpu.SemaphoreType.REGULAR,
             ],
             compiler_params=pltpu.CompilerParams(
                 collective_id=0, has_side_effects=True, vmem_limit_bytes=VMEM_BYTES

time: 24.6 us -> 22.8 us (0.927)
  the two profiles are of different devices: /device:TPU:4 before, /device:TPU:2 now
where the time goes in v7:
time: 22.8 us; the launch traced here: 22.6 us
  Pallas kernels  21.9 us (96%)
  local copies, waits for them, and re-layouts  0.71 us (3%)
    pallas_call x1, Pallas kernels, body(): pl.pallas_call(functools.partial(kernel, count), out_shape=jax.ShapeDtype...  21.9 us
    unnamed x1, local copies, waits for them, and re-layouts  0.71 us

profile of v7, /device:TPU:2, one launch (start us, length us, event | category | flops | bytes accessed | tf_op | source)
XLA Modules:
  0.0 22.6 jit_solution(2689076330207832509)
XLA Ops:
  0.0 21.9 %shard_map.28 = f32[256,256]{1,0:T(8,128)S(1)} custom-call(f32[2,1024,256]{2,1,0:T(8,128)} %x_ref.1, bf16[3920,640]{1,0:T(8,128)(2,1)} %constant.2.clone.const_ref), custom_call_target="tpu_custom_call" | custom-call | tf_op jit(solution)/shard_map/pallas_call | solution.py:616
  21.9 0.7 %copy.4 = f32[256,256]{1,0:T(8,128)} copy(f32[256,256]{1,0:T(8,128)S(1)} %shard_map.28) | data formatting | bytes 524288

commit v8 on v7

--- a/solution.py
+++ b/solution.py
@@ -25,9 +25,9 @@
 SUB = 64
 SUBS = BLOCK // SUB
 EXT = 67
-WIDE = 640
-ROW_PART = MID + LOW + BLOCK
-COL_PART = 2 * 256
+WIDE = 512
+ROW_PART = LOW + BLOCK
+COL_PART = 2 * 256 + 128
 REST = 4 * ROW_PART + 3 * COL_PART
 LATE = KEEP2 + SUB // 2
 EDGE = 76
@@ -35,7 +35,10 @@
 TO_RIGHT = 72
 TO_LEFT = 80
 PART = 48
-OWN = 48
+OWN = 32
+TOP = 16
+BOTTOM = 32
+P_SIZE = 8
 GATE = 1
 EXPO = float(-4.0 * np.log2(np.e))
 
@@ -76,13 +79,10 @@
 
 @functools.lru_cache(None)
 def matrices():
-    r0, r1 = reduce_matrix(ROWS), reduce_matrix(ROWS // 2)
+    r1 = reduce_matrix(ROWS // 2)
     e0 = expand_matrix(ROWS // 2)
-    row_in, row_low, row_up = [], [], []
+    row_low, row_up = [], []
     for p in range(4):
-        start = min(max(BLOCK * p - 16, 0), ROWS - WIN)
-        m = window(r0, 128 * p - 4, MID, start, WIN)
-        row_in.append(np.concatenate([m, m], 1))
         m = window(r1, 64 * p - 2, LOW, 128 * p - 4, MID)
         row_low.append(np.concatenate([m, m], 1))
         m = window(e0, BLOCK * p, BLOCK, 128 * p - 4, MID)
@@ -91,6 +91,8 @@
     row_sub = np.concatenate([m, m], 1)
     m = window(expand_matrix(ROWS // 4), 124, MID, 62, LOW)
     row_base = np.concatenate([m, m], 1)
+    row_both = [up[:, :MID] @ m for up in row_up]
+    row_up = [np.concatenate([up, np.concatenate([v, v], 1)], 1) for up, v in zip(row_up, row_both)]
     n = 3 * COLS
     c0, c1 = reduce_matrix(n), reduce_matrix(n // 2)
     x0 = expand_matrix(n // 2)
@@ -135,9 +137,10 @@
     col_base[:67, :128] = window(base, 128, 128, 63, 67).T
     col_base[:67, 128 + EXT] = window(base, 127, 1, 63, 67)[0]
     col_base[:67, 128 + EXT + 1] = window(base, 256, 1, 63, 67)[0]
+    col_up = [np.concatenate([up, col_base @ up / P_SIZE], 0) for up in col_up]
     parts = []
     for p in range(4):
-        parts += [row_in[p], row_low[p], row_up[p]]
+        parts += [row_low[p], row_up[p]]
     for b in range(3):
         parts += [col_in[b], col_up[b]]
     parts += [col_base, row_base, row_sub, col_halo]
@@ -171,7 +174,7 @@
     count,
     x_ref, const_ref,
     out_ref,
-    xwin, xpart, m_row_part, m_row_in, m_row_low, m_row_up, m_row_sub, m_row_base, m_col_in, m_col_halo, m_col_up, m_col_base,
+    xwin, xpart, m_row_low, m_row_up, m_row_sub, m_row_base, m_col_in, m_col_halo, m_col_up, m_col_base,
     keep, pack, halo, wide, c1, low, part, part_in,
     level0, level1, late, far0, far1, far_late, jbuf, upper,
     m_sem, x_sem, part_send, part_recv, swap_send, swap_recv, halo_send, halo_recv, far_send, far_recv, group_sem, sibling_sem, far_sem, beside_sem,
@@ -208,40 +211,48 @@
     def offset_of(p):
         return pl.multiple_of(16 - 16 * ((3 - p) // 3) + 16 * (p // 3), 16)
 
+    def half(ref, h):
+        return ref.at[:, :, pl.ds(128 * h, 128)]
+
     own = []
     for b in range(2):
-        own.append(
-            pltpu.make_async_copy(
-                x_ref.at[:, pl.ds(start_of(blocks[b]), WIN)], xwin.at[b, pl.ds(0, 2)], x_sem.at[b]
+        for h in range(2):
+            own.append(
+                pltpu.make_async_copy(
+                    half(x_ref.at[:, pl.ds(start_of(blocks[b]), WIN)], h),
+                    xwin.at[b, pl.ds(0, 2), h, pl.ds(TOP, WIN)],
+                    x_sem.at[b, h],
+                )
             )
-        )
 
     def const(at, rows, cols):
         return const_ref.at[pl.ds(pl.multiple_of(at, 16), rows), pl.ds(0, cols)]
 
     col_at = 4 * ROW_PART + COL_PART * side
     loads = [
-        (const(ROW_PART * far, MID, WIDE), m_row_in.at[0]),
-        (const(ROW_PART * me, MID, WIDE), m_row_in.at[1]),
         (const(col_at, 256, 512), m_col_in),
         (const(REST + 128 + MID, SUB, 128), m_row_sub),
-        (const(ROW_PART * far + MID, LOW, 384), m_row_low.at[0]),
+        (const(ROW_PART * far, LOW, 384), m_row_low.at[0]),
         (const(REST, 128, 256), m_col_base),
         (const(REST + 128, MID, 256), m_row_base),
         (const(REST + 128 + MID + SUB, 128, 512), m_col_halo),
-        (const(ROW_PART * me + MID, LOW, 384), m_row_low.at[1]),
-        (const(col_at + 256, 256, 256), m_col_up),
-        (const(ROW_PART * me + MID + LOW, BLOCK, 384), m_row_up),
-        (const(ROW_PART * first, PART, 128), m_row_part),
+        (const(ROW_PART * me, LOW, 384), m_row_low.at[1]),
+        (const(col_at + 256, 256 + 128, 256), m_col_up),
+        (const(ROW_PART * me + LOW, BLOCK, 512), m_row_up),
     ]
     loads = [pltpu.make_async_copy(s, d, m_sem.at[i]) for i, (s, d) in enumerate(loads)]
-    early = pltpu.make_async_copy(x_ref.at[:, pl.ds(start_of(first), 128)], xpart, x_sem.at[2])
-    early.start()
-    loads[11].start()
-    loads[2].start()
-    loads[3].start()
+    early = [
+        pltpu.make_async_copy(
+            half(x_ref.at[:, pl.ds(start_of(first), 128)], h), xpart.at[:, h, pl.ds(TOP, 128)], x_sem.at[2, h]
+        )
+        for h in range(2)
+    ]
+    early[0].start()
+    early[1].start()
+    loads[0].start()
+    loads[1].start()
     own[0].start()
-    loads[0].start()
+    own[1].start()
 
     def twice(ref):
         m = ref[...]
@@ -273,25 +284,32 @@
 
     swaps = []
     for b, p in enumerate((far_sibling, sibling)):
-        swaps.append(
-            remote(
-                x_ref.at[:, pl.ds(start_of(p), WIN)],
-                xwin.at[b, pl.ds(2, 2)],
-                swap_send.at[b],
-                swap_recv.at[b],
-                sibling,
-                q,
+        for h in range(2):
+            swaps.append(
+                remote(
+                    half(x_ref.at[:, pl.ds(start_of(p), WIN)], h),
+                    xwin.at[b, pl.ds(2, 2), h, pl.ds(TOP, WIN)],
+                    swap_send.at[b, h],
+                    swap_recv.at[b, h],
+                    sibling,
+                    q,
+                )
             )
-        )
+
     @pl.when(core == 1)
     def _():
         pl.semaphore_wait(sibling_sem, 1)
 
     swaps[0].start()
-
-    own[1].start()
-    loads[1].start()
-    for copy in loads[4:11]:
+    swaps[1].start()
+
+    for b in range(2):
+        for p in range(4):
+            xwin[b, p, :, pl.ds(0, TOP)] = jnp.zeros((2, TOP, 128), F32)
+            xwin[b, p, :, pl.ds(TOP + WIN, BOTTOM)] = jnp.zeros((2, BOTTOM, 128), F32)
+    own[2].start()
+    own[3].start()
+    for copy in loads[2:]:
         copy.start()
     jbuf[pl.ds(KEEP, MID - KEEP)] = jnp.zeros((MID - KEEP, COLS), F32)
 
@@ -303,19 +321,33 @@
     def _():
         halo[1] = jnp.zeros((MID // 3, 128), F32)
 
-    early.wait()
-    for i in (11, 2, 3):
-        loads[i].wait()
+    def joined(ref, at, rows):
+        return jnp.concatenate([ref[at + (0, rows)], ref[at + (1, rows)]], 1)
+
+    def rows_down(ref, at, block, rows):
+        base = offset_of(block) + TOP - 10
+        taps = [joined(ref, at, pl.ds(base + t, rows, stride=2)) for t in range(5)]
+        value = (taps[0] + taps[4]) * TAPS[0] + (taps[1] + taps[3]) * TAPS[1] + taps[2] * TAPS[2]
+        row = lax.broadcasted_iota(jnp.int32, (rows, COLS), 0)
+        inside = (row >= 4 * ((3 - block) // 3)) & (row < MID - 12 * (block // 3))
+        return jnp.where(inside, value, 0.0)
+
+    for p in range(2):
+        xpart[p, :, pl.ds(0, TOP)] = jnp.zeros((2, TOP, 128), F32)
+
+    early[0].wait()
+    early[1].wait()
+    loads[0].wait()
+    loads[1].wait()
     num = jnp.zeros((OWN, COLS), F32)
     den = jnp.zeros((OWN, COLS), F32)
     for p in range(2):
-        m = m_row_part[...]
-        value = dot(jnp.concatenate([m, m], 1), tall(xpart[p]))
+        value = rows_down(xpart, (p,), first, PART)
         m = m_col_in[:, pl.ds(0, COLS)]
         value = dot(jnp.concatenate(split(value), 0), m)
         value = value[:PART] + value[PART:]
         z = dot(m_row_sub[pl.ds(0, OWN), pl.ds(0, 2 * PART)], tall(value))
-        d = xpart[p, pl.ds(offset_of(first), OWN)] - z
+        d = joined(xpart, (p,), pl.ds(pl.multiple_of(TOP + offset_of(first), 16), OWN)) - z
         w = weight(d)
         num = num + w * d
         den = den + w
@@ -329,7 +361,8 @@
         pl.semaphore_wait(far_sem, 1)
 
     far_part.start()
-    swaps[1].start()
+    swaps[2].start()
+    swaps[3].start()
 
     @pl.when(me == GATE)
     def _():
@@ -366,11 +399,12 @@
 
     def rows_in(b, p):
         if p == 0:
-            own[b].wait()
-            loads[b].wait()
+            own[2 * b].wait()
+            own[2 * b + 1].wait()
         if p == 2:
-            swaps[b].wait_recv()
-        return dot(m_row_in[b, :, pl.ds(0, 2 * WIN)], tall(xwin[b, p]))
+            swaps[2 * b].wait_recv()
+            swaps[2 * b + 1].wait_recv()
+        return rows_down(xwin, (b, p), blocks[b], MID)
 
     def columns_in(b, planes):
         halves = []
@@ -394,7 +428,7 @@
             rows = pl.ds(32 * s, 48)
             both = jnp.concatenate([wide[p, 0, rows], wide[p, 1, rows]], 0)
             z = dot(m_row_sub[:, pl.ds(0, 96)], both)
-            d = xwin[b, p, pl.ds(pl.multiple_of(offset_of(blocks[b]) + SUB * s, 16), SUB)] - z
+            d = joined(xwin, (b, p), pl.ds(pl.multiple_of(TOP + offset_of(blocks[b]) + SUB * s, 16), SUB)) - z
             w = weight(d)
             num = num + w * d
             den = den + w
@@ -493,7 +527,7 @@
     for s in range(SUBS - 1):
         pl.when(core == 0)(far_zero[s].start)
     far_chunk(SUBS - 1)
-    for copy in loads[4:7]:
+    for copy in loads[2:5]:
         copy.wait()
     num, den, _ = sums_one(0)
     put_one(0, num, den)
@@ -503,7 +537,7 @@
     pl.when(ahead)(send_halo)
 
     pl.when(behind)(far_zero[SUBS - 1].start)
-    for copy in loads[7:11]:
+    for copy in loads[5:]:
         copy.wait()
 
     @pl.when(has_left)
@@ -554,21 +588,23 @@
     own_tile, far_tile = late[1, pl.ds(0, KEEP2)], far_late[pl.ds(0, KEEP2)]
     tile = own_tile + far_tile
     total = jnp.concatenate([jnp.where(low_lane < EXT, tile, 0.0), jnp.zeros((LOW - KEEP2, 128), F32)], 0)
-    base = dot(m_row_base[:, pl.ds(0, 2 * LOW)], tall(columns_up(total)))
+    coarse = m_col_up[pl.ds(256, 128)]
+    base = dot(jnp.concatenate(split(total), 1), jnp.concatenate([coarse, coarse], 0))
     at_edge = (keep_lane < 6) | (keep_lane >= 124)
     sums = []
     for i in range(2):
         at = EDGE + 20 * i
         edges = jnp.concatenate([turn(far_tile, -(4 + at))[:64], turn(far_tile, -(14 + at))], 0)
         sums.append(level1[1, i] + jnp.where(at_edge, edges, far1[i]))
-    jbuf[pl.ds(0, KEEP), pl.ds(0, 128)] = sums[0] * inverse(sums[1]) + base[:KEEP, :128] * 0.125
+    jbuf[pl.ds(0, KEEP), pl.ds(0, 128)] = sums[0] * inverse(sums[1])
     outer = (low_lane >= EXT) & (low_lane < EXT + 4)
     ratio = jnp.where(outer, tile, 0.0) * inverse(jnp.where(outer, turn(tile, -4), 1.0))
-    ratio = jnp.concatenate([ratio[:64], turn(ratio, -2)], 0) + base[:KEEP, 128:] * 0.125
+    ratio = jnp.concatenate([ratio[:64], turn(ratio, -2)], 0)
     ratio = jnp.where((keep_lane >= EXT) & (keep_lane < EXT + 2), ratio, 0.0)
     jbuf[pl.ds(0, KEEP), pl.ds(128, 128)] = ratio
-    u = dot(jnp.concatenate(split(jbuf[...]), 1), twice(m_col_up))
-    upper[...] = dot(m_row_up[:, pl.ds(0, 2 * MID)], tall(u))
+    m = m_col_up[pl.ds(0, 256)]
+    u = dot(jnp.concatenate(split(jbuf[...]), 1), jnp.concatenate([m, m], 0))
+    upper[...] = dot(m_row_up[:, pl.ds(0, 2 * (MID + LOW))], jnp.concatenate([tall(u), tall(base)], 0))
 
     @pl.when(core == 1)
     def _():
@@ -619,17 +655,15 @@
             in_specs=[pl.BlockSpec(memory_space=pl.ANY)] * 2,
             out_specs=pl.BlockSpec(memory_space=pltpu.VMEM),
             scratch_shapes=[
-                vmem((2, 4, WIN, COLS), F32),
-                vmem((2, 128, COLS), F32),
-                vmem((PART, 128), BF),
-                vmem((2, MID, WIDE), BF),
+                vmem((2, 4, 2, TOP + WIN + BOTTOM, 128), F32),
+                vmem((2, 2, TOP + 128, 128), F32),
                 vmem((2, LOW, 384), BF),
-                vmem((BLOCK, 384), BF),
+                vmem((BLOCK, 512), BF),
                 vmem((SUB, 128), BF),
                 vmem((MID, 256), BF),
                 vmem((256, 512), BF),
                 vmem((128, 512), BF),
-                vmem((256, 256), BF),
+                vmem((384, 256), BF),
                 vmem((128, 256), BF),
                 vmem((2, 4, MID, 512), F32),
                 vmem((2, MID // 3, 128), F32),
@@ -647,12 +681,12 @@
                 vmem((LATE, 128), F32),
                 vmem((MID, COLS), F32),
                 vmem((BLOCK, COLS), F32),
-                dma((12,)),
-                dma((3,)),
+                dma((9,)),
+                dma((3, 2)),
                 dma((1,)),
                 dma((2,)),
-                dma((2,)),
-                dma((2,)),
+                dma((2, 2)),
+                dma((2, 2)),
                 dma((2,)),
                 dma((2,)),
                 dma((SUBS + 2,)),

time: 22.8 us -> 22.5 us (0.987)
  no operation moved by 1% of the time
where the time goes in v8:
time: 22.5 us; the launch traced here: 22.4 us
  Pallas kernels  21.7 us (96%)
  local copies, waits for them, and re-layouts  0.71 us (3%)
    pallas_call x1, Pallas kernels, body(): pl.pallas_call(functools.partial(kernel, count), out_shape=jax.ShapeDtype...  21.7 us
    unnamed x1, local copies, waits for them, and re-layouts  0.71 us

profile of v8, /device:TPU:2, one launch (start us, length us, event | category | flops | bytes accessed | tf_op | source)
XLA Modules:
  0.0 22.4 jit_solution(4388421924725603888)
XLA Ops:
  0.0 21.7 %shard_map.28 = f32[256,256]{1,0:T(8,128)S(1)} custom-call(f32[2,1024,256]{2,1,0:T(8,128)} %x_ref.1, bf16[3728,512]{1,0:T(8,128)(2,1)} %constant.2.clone.const_ref), custom_call_target="tpu_custom_call" | custom-call | tf_op jit(solution)/shard_map/pallas_call | solution.py:652
  21.7 0.7 %copy.4 = f32[256,256]{1,0:T(8,128)} copy(f32[256,256]{1,0:T(8,128)S(1)} %shard_map.28) | data formatting | bytes 524288

commit v9 on v8

--- a/solution.py
+++ b/solution.py
@@ -476,7 +476,6 @@
     columns_in(0, (0, 1))
     put(0, keep[0, 0])
     put(1, keep[0, 1])
-    columns_in(1, (0, 1))
     columns_in(0, (2, 3))
     put(2, keep[0, 2])
     put(3, keep[0, 3])
@@ -492,6 +491,7 @@
     far_chunk(0)
     pl.when(core == 1)(far_rest.start)
     pl.when(jnp.logical_not(ahead))(meet)
+    columns_in(1, (0, 1))
     columns_in(1, (2, 3))
     packs = [jnp.zeros((MID // 3, 128), F32), jnp.zeros((MID // 3, 128), F32)]
     for b in range(2):
@@ -524,14 +524,14 @@
 
     pl.when(jnp.logical_not(ahead))(send_halo)
 
-    for s in range(SUBS - 1):
-        pl.when(core == 0)(far_zero[s].start)
     far_chunk(SUBS - 1)
     for copy in loads[2:5]:
         copy.wait()
     num, den, _ = sums_one(0)
     put_one(0, num, den)
     far_one.start()
+    for s in range(SUBS - 1):
+        pl.when(core == 0)(far_zero[s].start)
 
     pl.when(ahead)(meet)
     pl.when(ahead)(send_halo)

time: 22.5 us -> 22.5 us (level)
  no operation moved by 1% of the time
where the time goes in v9:
time: 22.5 us; the launch traced here: 22.4 us
  Pallas kernels  21.7 us (96%)
  local copies, waits for them, and re-layouts  0.71 us (3%)
    pallas_call x1, Pallas kernels, body(): pl.pallas_call(functools.partial(kernel, count), out_shape=jax.ShapeDtype...  21.7 us
    unnamed x1, local copies, waits for them, and re-layouts  0.71 us

profile of v9, /device:TPU:2, one launch (start us, length us, event | category | flops | bytes accessed | tf_op | source)
XLA Modules:
  0.0 22.4 jit_solution(12186229878813275697)
XLA Ops:
  0.0 21.7 %shard_map.28 = f32[256,256]{1,0:T(8,128)S(1)} custom-call(f32[2,1024,256]{2,1,0:T(8,128)} %x_ref.1, bf16[3728,512]{1,0:T(8,128)(2,1)} %constant.2.clone.const_ref), custom_call_target="tpu_custom_call" | custom-call | tf_op jit(solution)/shard_map/pallas_call | solution.py:652
  21.7 0.7 %copy.4 = f32[256,256]{1,0:T(8,128)} copy(f32[256,256]{1,0:T(8,128)S(1)} %shard_map.28) | data formatting | bytes 524288

commit v10 on v9

--- a/solution.py
+++ b/solution.py
@@ -468,14 +468,20 @@
                 tile = jnp.where(low_lane >= at, turn(v[64 * h : 64 * h + KEEP2, :128], 4 + at), tile)
         return tile
 
-    far_zero = [remote(level0.at[0, s], far0.at[s], far_send.at[s], far_recv.at[s], far, q) for s in range(SUBS)]
+    far_zero = [remote(level0.at[0, s], far0.at[s], far_send.at[s], far_recv.at[s], far, q) for s in range(SUBS - 1)]
+    far_ends = []
+    for i in range(2):
+        rows = pl.ds(SUB // 2 * i, SUB // 2)
+        src, dst, at = level0.at[0, SUBS - 1, :, rows], far0.at[SUBS - 1, :, rows], SUBS + 2 * i
+        far_ends.append(remote(src, dst, far_send.at[at], far_recv.at[at], far, q))
     rest = pl.ds(OWN, SUB - OWN)
     far_rest = remote(level0.at[0, 0, :, rest], far0.at[0, :, rest], far_send.at[0], far_recv.at[0], far, q)
-    far_one = remote(level1.at[0], far1, far_send.at[SUBS], far_recv.at[SUBS], far, q)
+    far_one = remote(level1.at[0], far1, far_send.at[SUBS - 1], far_recv.at[SUBS - 1], far, q)
     far_last = remote(late.at[0], far_late, far_send.at[SUBS + 1], far_recv.at[SUBS + 1], far, q)
     columns_in(0, (0, 1))
     put(0, keep[0, 0])
     put(1, keep[0, 1])
+    columns_in(1, (0, 1))
     columns_in(0, (2, 3))
     put(2, keep[0, 2])
     put(3, keep[0, 3])
@@ -491,7 +497,6 @@
     far_chunk(0)
     pl.when(core == 1)(far_rest.start)
     pl.when(jnp.logical_not(ahead))(meet)
-    columns_in(1, (0, 1))
     columns_in(1, (2, 3))
     packs = [jnp.zeros((MID // 3, 128), F32), jnp.zeros((MID // 3, 128), F32)]
     for b in range(2):
@@ -525,6 +530,7 @@
     pl.when(jnp.logical_not(ahead))(send_halo)
 
     far_chunk(SUBS - 1)
+    pl.when(behind)(far_ends[0].start)
     for copy in loads[2:5]:
         copy.wait()
     num, den, _ = sums_one(0)
@@ -536,7 +542,6 @@
     pl.when(ahead)(meet)
     pl.when(ahead)(send_halo)
 
-    pl.when(behind)(far_zero[SUBS - 1].start)
     for copy in loads[5:]:
         copy.wait()
 
@@ -581,7 +586,8 @@
         if b == 0:
             late[0, pl.ds(KEEP2, SUB // 2)] = patch
             far_last.start()
-            pl.when(jnp.logical_not(behind))(far_zero[SUBS - 1].start)
+            pl.when(jnp.logical_not(behind))(far_ends[0].start)
+            far_ends[1].start()
 
     far_one.wait_recv()
     far_last.wait_recv()
@@ -616,7 +622,10 @@
     pl.when(core == 0)(far_zero[0].wait_recv)
     patch = far_late[pl.ds(KEEP2, SUB // 2)]
     for s in range(SUBS):
-        if s:
+        if s == SUBS - 1:
+            far_ends[0].wait_recv()
+            far_ends[1].wait_recv()
+        elif s:
             far_zero[s].wait_recv()
         sums = []
         for i in range(2):
@@ -638,7 +647,7 @@
 
     pl.when(core == 0)(far_zero[0].wait_send)
     pl.when(core == 1)(far_rest.wait_send)
-    for copy in swaps + far_zero[1:] + [far_one, far_last, far_part]:
+    for copy in swaps + far_zero[1:] + far_ends + [far_one, far_last, far_part]:
         copy.wait_send()
 
 
@@ -689,8 +698,8 @@
                 dma((2, 2)),
                 dma((2,)),
                 dma((2,)),
-                dma((SUBS + 2,)),
-                dma((SUBS + 2,)),
+                dma((SUBS + 3,)),
+                dma((SUBS + 3,)),
                 pltpu.SemaphoreType.REGULAR,
                 pltpu.SemaphoreType.REGULAR,
                 pltpu.SemaphoreType.REGULAR,

time: 22.5 us -> 22.5 us (level)
  no operation moved by 1% of the time
where the time goes in v10:
time: 22.5 us; the launch traced here: 22.4 us
  Pallas kernels  21.7 us (96%)
  local copies, waits for them, and re-layouts  0.71 us (3%)
    pallas_call x1, Pallas kernels, body(): pl.pallas_call(functools.partial(kernel, count), out_shape=jax.ShapeDtype...  21.7 us
    unnamed x1, local copies, waits for them, and re-layouts  0.71 us

profile of v10, /device:TPU:2, one launch (start us, length us, event | category | flops | bytes accessed | tf_op | source)
XLA Modules:
  0.0 22.4 jit_solution(1882707938689292154)
XLA Ops:
  0.0 21.7 %shard_map.28 = f32[256,256]{1,0:T(8,128)S(1)} custom-call(f32[2,1024,256]{2,1,0:T(8,128)} %x_ref.1, bf16[3728,512]{1,0:T(8,128)(2,1)} %constant.2.clone.const_ref), custom_call_target="tpu_custom_call" | custom-call | tf_op jit(solution)/shard_map/pallas_call | solution.py:661
  21.7 0.7 %copy.4 = f32[256,256]{1,0:T(8,128)} copy(f32[256,256]{1,0:T(8,128)S(1)} %shard_map.28) | data formatting | bytes 524288
